TPU v7x, 128 devices: a whole 4x4x4 slice. The times are simulated.
128 devices in a mesh: pipe: 4 (over y), expert: 32 (over z, x, core).
Axes of the slice: x: 4, y: 4, z: 4, core: 2. Of those that a mesh axis runs over, the one named last changes fastest.
Arguments:
- forward_input: bfloat16 [4, 4096, 3584], P('pipe', 'expert'), may hold values from -45 to 45
- forward_routes: int32 [4, 4096, 2], P('pipe', 'expert'), may hold values from 0 to 31, as said below
- forward_gates: float32 [4, 4096, 2], P('pipe', 'expert'), may hold values from 0.3 to 3
- backward_input: bfloat16 [4, 4096, 3584], P('pipe', 'expert'), may hold values from -45 to 45
- backward_routes: int32 [4, 4096, 2], P('pipe', 'expert'), may hold values from 0 to 31, as said below
- backward_gates: float32 [4, 4096, 2], P('pipe', 'expert'), may hold values from 0.3 to 3
- upstream_gradient: bfloat16 [4, 4096, 3584], P('pipe', 'expert'), may hold values from -6 to 6
- norm_gain: bfloat16 [4, 3584], P('pipe'), may hold values from 0.5 to 2
- gate_weight: bfloat16 [4, 32, 3584, 1024], P('pipe', 'expert'), may hold values from -0.09375 to 0.09375
- up_weight: bfloat16 [4, 32, 3584, 1024], P('pipe', 'expert'), may hold values from -0.09375 to 0.09375
- down_weight: bfloat16 [4, 32, 1024, 3584], P('pipe', 'expert'), may hold values from -0.1875 to 0.1875
Outputs:
- forward_next: bfloat16 [4, 4096, 3584], P('pipe', 'expert')
- backward_next: bfloat16 [4, 4096, 3584], P('pipe', 'expert')
Inputs may be any that keep to these rules, and one draw needn't show every extreme that they name: `forward_routes`: each token names 2 different experts. At every section, of the 128 tokens of one device at most 14 name any one expert, and one expert of the section is named by exactly 14 tokens of every device. `backward_routes`: each token names 2 different experts. At every section, of the 128 tokens of one device at most 14 name any one expert, and one expert of the section is named by exactly 14 tokens of every device.
All inputs are finite; a program needn't handle non-finite values.
Results may differ from a plain program's by a relative error of at most 0.0069.
Values may be sent and summed in bfloat16 or wider, within the bound.
A program may use at most 128 MiB of HBM per device.

v0:
```python
import jax
import jax.numpy as jnp
from jax import lax
from jax.sharding import PartitionSpec as P

EPSILON = 1e-06


def passed_along(array, axis, by):
    devices = lax.axis_size(axis)
    return lax.ppermute(array, axis, [(i, (i + by) % devices) for i in range(devices)])


def normalize(block, gain_row):
    values = block.astype(jnp.float32)
    inverse_rms = lax.rsqrt(jnp.mean(values * values, axis=-1, keepdims=True) + EPSILON)
    normed = (values * inverse_rms * gain_row.astype(jnp.float32)).astype(jnp.bfloat16)
    return (values, inverse_rms, normed)


def route_layout(choices_of, groups, capacity):
    tokens, fanout = choices_of.shape
    routes_all = tokens * fanout
    expert_of = choices_of.reshape(routes_all)
    onehot = (expert_of[:, None] == jnp.arange(groups, dtype=jnp.int32)[None, :]).astype(jnp.int32)
    position = jnp.sum((jnp.cumsum(onehot, axis=0) - onehot) * onehot, axis=1)
    slot_index = expert_of * capacity + position
    source = jnp.full((groups * capacity,), routes_all, jnp.int32)
    source = source.at[slot_index].set(jnp.arange(routes_all, dtype=jnp.int32))
    return (slot_index, source)


def pack_rows(block, source, groups, capacity):
    padded = jnp.concatenate([block, jnp.zeros((1, block.shape[1]), block.dtype)], axis=0)
    return padded[source].reshape(groups, capacity, block.shape[1])


def unpack_rows(returned, slot_index, tokens, fanout):
    features = returned.shape[-1]
    return (
        returned.reshape(-1, features)[slot_index]
        .reshape(tokens, fanout, features)
        .astype(jnp.float32)
    )


def expert_forward(block, gate_matrix, up_matrix, down_matrix):
    gate_pre = jnp.dot(block, gate_matrix, preferred_element_type=jnp.float32)
    up_pre = jnp.dot(block, up_matrix, preferred_element_type=jnp.float32)
    active = (gate_pre * jax.nn.sigmoid(gate_pre) * up_pre).astype(jnp.bfloat16)
    return jnp.dot(active, down_matrix, preferred_element_type=jnp.float32).astype(jnp.bfloat16)


def expert_backward(block, grads, gate_matrix, up_matrix, down_matrix):
    gate_pre = jnp.dot(block, gate_matrix, preferred_element_type=jnp.float32)
    up_pre = jnp.dot(block, up_matrix, preferred_element_type=jnp.float32)
    sigmoid_gate = jax.nn.sigmoid(gate_pre)
    hidden = jnp.einsum("md,fd->mf", grads, down_matrix, preferred_element_type=jnp.float32)
    gate_grad = (hidden * up_pre * sigmoid_gate * (1.0 + gate_pre * (1.0 - sigmoid_gate))).astype(
        jnp.bfloat16
    )
    up_grad = (hidden * gate_pre * sigmoid_gate).astype(jnp.bfloat16)
    summed = jnp.einsum("mf,df->md", gate_grad, gate_matrix, preferred_element_type=jnp.float32)
    summed = summed + jnp.einsum(
        "mf,df->md", up_grad, up_matrix, preferred_element_type=jnp.float32
    )
    return summed.astype(jnp.bfloat16)


def local(
    forward_input,
    forward_routes,
    forward_gates,
    backward_input,
    backward_routes,
    backward_gates,
    upstream_gradient,
    norm_gain,
    gate_weight,
    up_weight,
    down_weight,
):
    groups = lax.axis_size("expert")
    tokens = forward_routes.shape[1]
    fanout = forward_routes.shape[2]
    features = forward_input.shape[2]
    capacity = 7 * tokens * fanout // (4 * groups)
    gain_row = norm_gain[0]
    gate_matrix = gate_weight[0, 0]
    up_matrix = up_weight[0, 0]
    down_matrix = down_weight[0, 0]
    values, inverse_rms, normed = normalize(forward_input[0], gain_row)
    forward_slot, forward_source = route_layout(forward_routes[0], groups, capacity)
    forward_send = pack_rows(normed, forward_source // fanout, groups, capacity)
    stored, stored_rms, stored_normed = normalize(backward_input[0], gain_row)
    backward_slot, backward_source = route_layout(backward_routes[0], groups, capacity)
    grad_out = upstream_gradient[0].astype(jnp.float32)
    route_grad = (
        (backward_gates[0][:, :, None] * grad_out[:, None, :])
        .astype(jnp.bfloat16)
        .reshape(tokens * fanout, features)
    )
    stored_send = pack_rows(stored_normed, backward_source // fanout, groups, capacity)
    grad_send = pack_rows(route_grad, backward_source, groups, capacity)
    forward_got = lax.all_to_all(forward_send, "expert", split_axis=0, concat_axis=0, tiled=True)
    forward_out = expert_forward(
        forward_got.reshape(groups * capacity, features), gate_matrix, up_matrix, down_matrix
    )
    forward_back = lax.all_to_all(
        forward_out.reshape(groups, capacity, features),
        "expert",
        split_axis=0,
        concat_axis=0,
        tiled=True,
    )
    stored_got, grad_got = (
        lax.all_to_all(stored_send, "expert", split_axis=0, concat_axis=0, tiled=True),
        lax.all_to_all(grad_send, "expert", split_axis=0, concat_axis=0, tiled=True),
    )
    backward_out = expert_backward(
        stored_got.reshape(groups * capacity, features),
        grad_got.reshape(groups * capacity, features),
        gate_matrix,
        up_matrix,
        down_matrix,
    )
    backward_back = lax.all_to_all(
        backward_out.reshape(groups, capacity, features),
        "expert",
        split_axis=0,
        concat_axis=0,
        tiled=True,
    )
    picked = unpack_rows(forward_back, forward_slot, tokens, fanout)
    mixed = (values + jnp.sum(forward_gates[0][:, :, None] * picked, axis=1)).astype(jnp.bfloat16)
    forward_next = passed_along(mixed, "pipe", 1)
    picked_back = unpack_rows(backward_back, backward_slot, tokens, fanout)
    normed_grad = gain_row.astype(jnp.float32) * jnp.sum(picked_back, axis=1)
    cubed = stored_rms * stored_rms * stored_rms
    layer_grad = (
        grad_out
        + stored_rms * normed_grad
        - stored * cubed * jnp.mean(stored * normed_grad, axis=-1, keepdims=True)
    )
    backward_next = passed_along(layer_grad.astype(jnp.bfloat16), "pipe", -1)
    return (forward_next[None], backward_next[None])


def solution(mesh):
    in_specs = (
        P("pipe", "expert", None),
        P("pipe", "expert", None),
        P("pipe", "expert", None),
        P("pipe", "expert", None),
        P("pipe", "expert", None),
        P("pipe", "expert", None),
        P("pipe", "expert", None),
        P("pipe", None),
        P("pipe", "expert", None, None),
        P("pipe", "expert", None, None),
        P("pipe", "expert", None, None),
    )
    out_specs = (P("pipe", "expert", None), P("pipe", "expert", None))
    return jax.shard_map(local, mesh=mesh, in_specs=in_specs, out_specs=out_specs, check_vma=False)
```

profile of v0, /device:TPU:0, one launch (start us, length us, event | category | flops | bytes accessed | tf_op | source)
XLA Modules:
  0.0 430.7 jit_solution(451850932518545893)
XLA Ops:
  0.6 0.8 copy.21
  1.6 0.1 eq.58
  1.7 0.7 broadcast_multiply_fusion
  2.4 0.6 reduce-window.16
  3.0 0.2 slice_reduce_fusion
  3.3 0.1 mul.195
  3.6 1.4 scatter_custom_fusion.1
  5.0 1.4 fusion.21
  6.5 1.4 fusion.25
  7.9 0.8 convert_reduce_fusion
  8.7 1.5 fusion.27
  10.2 4.0 gather_fusion.3
  14.3 4.7 %reshape.181 = bf16[32,14,3584]{2,1,0:T(8,128)(2,1)} reshape(bf16[448,3584]{1,0:T(8,128)(2,1)} %gather_fusion.3) | data formatting | bytes 6422528 | tf_op jit(solution)/shard_map/reshape | solution.py:35
  18.9 8.5 %all-to-all-start.3 = ((bf16[32,14,3584]{2,1,0:T(8,128)(2,1)}), bf16[32,14,3584]{2,1,0:T(8,128)(2,1)}, u32[]{:S(2)}, u32[]{:S(2)}) async-start(bf16[32,14,3584]{2,1,0:T(8,128)(2,1)} %reshape.181), calls=%async_computation.3 | async-start | bytes 7340032 | tf_op jit(solution)/shard_map/all_to_all | solution.py:117
  27.4 0.2 bitcast_convert_fusion
  27.6 3.2 mul.191
  30.8 5.6 %mul.192 = f32[256,3584]{1,0:T(8,128)} reshape(f32[128,2,3584]{2,1,0:T(2,128)} %mul.191) | data formatting | bytes 7340032 | tf_op jit(solution)/shard_map/mul | solution.py:99
  36.7 2.4 multiply_convert_fusion
  39.2 4.1 gather_fusion.2
  43.3 4.7 %reshape.179 = bf16[32,14,3584]{2,1,0:T(8,128)(2,1)} reshape(bf16[448,3584]{1,0:T(8,128)(2,1)} %gather_fusion.2) | data formatting | bytes 6422528 | tf_op jit(solution)/shard_map/reshape | solution.py:35
  48.0 27.1 %all-to-all-done.3 = bf16[32,14,3584]{2,1,0:T(8,128)(2,1)} async-done(((bf16[32,14,3584]{2,1,0:T(8,128)(2,1)}), bf16[32,14,3584]{2,1,0:T(8,128)(2,1)}, u32[]{:S(2)}, u32[]{:S(2)}) %all-to-all-start.3) | async-done | bytes 3211296 | tf_op jit(solution)/shard_map/all_to_all | solution.py:117
  75.1 5.3 %all-to-all-start.2 = ((bf16[32,14,3584]{2,1,0:T(8,128)(2,1)}), bf16[32,14,3584]{2,1,0:T(8,128)(2,1)}, u32[]{:S(2)}, u32[]{:S(2)}) async-start(bf16[32,14,3584]{2,1,0:T(8,128)(2,1)} %reshape.179), calls=%async_computation.2 | async-start | bytes 7340032 | tf_op jit(solution)/shard_map/all_to_all | solution.py:118
  80.4 3.2 reshape.182
  83.6 7.0 %fusion.12 = f32[448,1024]{1,0:T(8,128)} fusion(bf16[448,3584]{1,0:T(8,128)(2,1)S(1)} %reshape.182, bf16[1,1,3584,1024]{3,2,1,0:T(8,128)(2,1)} %param.19), kind=kOutput, calls=%fused_computation.19 | convolution fusion | flops 3288334336 | bytes 12386304 | tf_op jit(solution)/shard_map/dot_general | solution.py:55
  90.6 37.5 %all-to-all-done.2 = bf16[32,14,3584]{2,1,0:T(8,128)(2,1)} async-done(((bf16[32,14,3584]{2,1,0:T(8,128)(2,1)}), bf16[32,14,3584]{2,1,0:T(8,128)(2,1)}, u32[]{:S(2)}, u32[]{:S(2)}) %all-to-all-start.2) | async-done | bytes 3211296 | tf_op jit(solution)/shard_map/all_to_all | solution.py:118
  128.1 4.7 %reshape.180 = bf16[448,3584]{1,0:T(8,128)(2,1)} reshape(bf16[32,14,3584]{2,1,0:T(8,128)(2,1)} %all-to-all-done.2) | data formatting | bytes 6422528 | tf_op jit(solution)/shard_map/reshape | solution.py:122
  132.8 6.9 %fusion = f32[448,1024]{1,0:T(8,128)S(1)} fusion(bf16[448,3584]{1,0:T(8,128)(2,1)} %reshape.180, bf16[1,1,1024,3584]{3,2,1,0:T(8,128)(2,1)} %param.21), kind=kOutput, calls=%fused_computation.7 | convolution fusion | flops 3288334336 | bytes 12386304 | tf_op jit(solution)/shard_map/md,fd->mf/dot_general | solution.py:58
  139.7 1.3 copy-done.9
  140.9 9.5 %fusion.4 = f32[448,3584]{1,0:T(8,128)} fusion(bf16[1,1,3584,1024]{3,2,1,0:T(8,128)(2,1)} %param.20, f32[448,1024]{1,0:T(8,128)S(1)} %fusion, f32[448,1024]{1,0:T(8,128)S(1)} %copy-done.8), kind=kOutput, calls=%fused_computation.11 | convolution fusion | flops 3291086848 | bytes 17432576 | tf_op jit(solution)/shard_map/mf,df->md/dot_general | solution.py:64
  150.4 16.9 %add_convert_fusion = bf16[448,3584]{1,0:T(8,128)(2,1)} fusion(f32[448,3584]{1,0:T(8,128)} %fusion.4, bf16[1,1,3584,1024]{3,2,1,0:T(8,128)(2,1)} %param.19, f32[448,1024]{1,0:T(8,128)} %fusion.12, f32[448,1024]{1,0:T(8,128)} %copy-done.9, bf16[448,3584]{1,0:T(8,128)(2,1)S(1)} %reshape.182, bf16[1,1,3584,1024]{3,2,1,0:T(8,128)(2,1)} %param.20), kind=kOutput, calls=%fused_computation.23 | convolution fusion | flops 6584467456 | bytes 31195136 | tf_op jit(solution)/shard_map/mf,df->md/dot_general | solution.py:63
  167.3 4.7 %reshape.183 = bf16[32,14,3584]{2,1,0:T(8,128)(2,1)} reshape(bf16[448,3584]{1,0:T(8,128)(2,1)} %add_convert_fusion) | data formatting | bytes 6422528 | tf_op jit(solution)/shard_map/reshape | solution.py:128
  172.0 5.0 %all-to-all-start.4 = ((bf16[32,14,3584]{2,1,0:T(8,128)(2,1)}), bf16[32,14,3584]{2,1,0:T(8,128)(2,1)}, u32[]{:S(2)}, u32[]{:S(2)}) async-start(bf16[32,14,3584]{2,1,0:T(8,128)(2,1)} %reshape.183), calls=%async_computation.4 | async-start | bytes 7340032 | tf_op jit(solution)/shard_map/all_to_all | solution.py:127
  177.4 0.6 reduce-window.14
  178.0 0.2 slice_reduce_fusion.1
  178.3 0.1 mul.182
  178.6 1.6 scatter_custom_fusion
  180.2 44.4 %all-to-all-done.4 = bf16[32,14,3584]{2,1,0:T(8,128)(2,1)} async-done(((bf16[32,14,3584]{2,1,0:T(8,128)(2,1)}), bf16[32,14,3584]{2,1,0:T(8,128)(2,1)}, u32[]{:S(2)}, u32[]{:S(2)}) %all-to-all-start.4) | async-done | bytes 3211296 | tf_op jit(solution)/shard_map/all_to_all | solution.py:127
  224.6 3.2 reshape.184
  227.8 3.0 gather_fusion.4
  230.8 5.2 %reshape.190 = f32[128,2,3584]{2,1,0:T(2,128)} reshape(bf16[256,3584]{1,0:T(8,128)(2,1)} %gather_fusion.4) | data formatting | bytes 5505024 | tf_op jit(solution)/shard_map/convert_element_type | solution.py:43
  236.0 6.5 %reduce_sum.74 = f32[128,3584]{1,0:T(8,128)S(1)} reduce(f32[128,2,3584]{2,1,0:T(2,128)} %reshape.190, f32[]{:T(128)} %constant.40.clone.1), dimensions={1}, to_apply=%region_11.12 | reduce | flops 458752 | bytes 5505028 | tf_op jit(solution)/shard_map/reduce_sum | solution.py:138
  242.5 0.3 fusion.31
  242.8 0.8 copy-done.1
  243.6 0.3 copy-done.4
  243.9 2.0 fusion.30
  246.0 4.1 gather_fusion
  250.1 4.7 %reshape.174 = bf16[32,14,3584]{2,1,0:T(8,128)(2,1)} reshape(bf16[448,3584]{1,0:T(8,128)(2,1)} %gather_fusion) | data formatting | bytes 6422528 | tf_op jit(solution)/shard_map/reshape | solution.py:35
  254.7 50.5 %all_to_all.25 = bf16[32,14,3584]{2,1,0:T(8,128)(2,1)} all-to-all(bf16[32,14,3584]{2,1,0:T(8,128)(2,1)} %reshape.174), channel_id=1, replica_groups=mesh['pipe'=4,'expert'=32] {'expert'}, dimensions={0} | all-to-all | bytes 6422528 | tf_op jit(solution)/shard_map/all_to_all | solution.py:105
  305.2 3.2 reshape.175
  308.4 7.0 %fusion.14 = f32[448,1024]{1,0:T(8,128)} fusion(bf16[448,3584]{1,0:T(8,128)(2,1)S(1)} %reshape.175, bf16[1,1,3584,1024]{3,2,1,0:T(8,128)(2,1)} %param.19), kind=kOutput, calls=%fused_computation.21 | convolution fusion | flops 3288334336 | bytes 12386304 | tf_op jit(solution)/shard_map/dot_general | solution.py:48
  315.5 14.3 %fusion.18 = bf16[448,3584]{1,0:T(8,128)(2,1)} fusion(bf16[1,1,1024,3584]{3,2,1,0:T(8,128)(2,1)} %param.21, f32[448,1024]{1,0:T(8,128)} %fusion.14, bf16[448,3584]{1,0:T(8,128)(2,1)S(1)} %reshape.175, bf16[1,1,3584,1024]{3,2,1,0:T(8,128)(2,1)} %param.20), kind=kOutput, calls=%fused_computation.24 | convolution fusion | flops 6581026816 | bytes 22937600 | tf_op jit(solution)/shard_map/dot_general | solution.py:51
  329.8 4.7 %reshape.176 = bf16[32,14,3584]{2,1,0:T(8,128)(2,1)} reshape(bf16[448,3584]{1,0:T(8,128)(2,1)} %fusion.18) | data formatting | bytes 6422528 | tf_op jit(solution)/shard_map/reshape | solution.py:110
  334.5 5.0 %all-to-all-start.1 = ((bf16[32,14,3584]{2,1,0:T(8,128)(2,1)}), bf16[32,14,3584]{2,1,0:T(8,128)(2,1)}, u32[]{:S(2)}, u32[]{:S(2)}) async-start(bf16[32,14,3584]{2,1,0:T(8,128)(2,1)} %reshape.176), calls=%async_computation.1 | async-start | bytes 7340032 | tf_op jit(solution)/shard_map/all_to_all | solution.py:109
  339.6 3.3 collective-permute-start.1
  342.9 44.2 %all-to-all-done.1 = bf16[32,14,3584]{2,1,0:T(8,128)(2,1)} async-done(((bf16[32,14,3584]{2,1,0:T(8,128)(2,1)}), bf16[32,14,3584]{2,1,0:T(8,128)(2,1)}, u32[]{:S(2)}, u32[]{:S(2)}) %all-to-all-start.1) | async-done | bytes 3211296 | tf_op jit(solution)/shard_map/all_to_all | solution.py:109
  387.1 3.2 reshape.177
  390.3 3.0 gather_fusion.1
  393.3 5.2 %reshape.187 = f32[128,2,3584]{2,1,0:T(2,128)} reshape(bf16[256,3584]{1,0:T(8,128)(2,1)} %gather_fusion.1) | data formatting | bytes 5505024 | tf_op jit(solution)/shard_map/convert_element_type | solution.py:43
  398.5 7.4 %multiply_reduce_fusion = f32[128,3584]{1,0:T(8,128)S(1)} fusion(f32[128,2,3584]{2,1,0:T(2,128)} %reshape.187, f32[128,2]{1,0:T(8,128)S(1)} %copy.14), kind=kLoop, calls=%fused_computation.26 | loop fusion | flops 1376256 | bytes 5506048 | tf_op jit(solution)/shard_map/reduce_sum | solution.py:135
  405.9 0.2 fusion.24
  406.0 1.6 collective-permute-start
  407.7 19.6 %collective-permute-done = bf16[128,3584]{1,0:T(8,128)(2,1)S(1)} collective-permute-done((bf16[128,3584]{1,0:T(8,128)(2,1)S(1)}, bf16[128,3584]{1,0:T(8,128)(2,1)S(1)}, u32[]{:S(2)}, u32[]{:S(2)}) %collective-permute-start) | collective-permute-done | bytes 917536 | tf_op jit(solution)/shard_map/ppermute | solution.py:11
  427.3 0.9 copy.30
  428.2 2.2 copy.31
  (51 shorter events, 1.8 us)
Async XLA Ops:
  18.9 8.5 %copy-start.3 = (bf16[1,128,3584]{2,1,0:T(8,128)(2,1)S(1)}, bf16[1,128,3584]{2,1,0:T(8,128)(2,1)}, u32[]{:S(2)}) copy-start(bf16[1,128,3584]{2,1,0:T(8,128)(2,1)} %param.17) | copy-start | bytes 2752516
  18.9 56.2 %all-to-all-start.3 = ((bf16[32,14,3584]{2,1,0:T(8,128)(2,1)}), bf16[32,14,3584]{2,1,0:T(8,128)(2,1)}, u32[]{:S(2)}, u32[]{:S(2)}) async-start(bf16[32,14,3584]{2,1,0:T(8,128)(2,1)} %reshape.181), calls=%async_computation.3 | async-start | bytes 7340032 | tf_op jit(solution)/shard_map/all_to_all | solution.py:117
  30.8 5.6 %copy-start.6 = (f32[1,128,2]{1,2,0:T(2,128)S(1)}, f32[1,128,2]{1,2,0:T(2,128)}, u32[]{:S(2)}) copy-start(f32[1,128,2]{1,2,0:T(2,128)} %param.16) | copy-start | bytes 3076
  75.1 53.0 %all-to-all-start.2 = ((bf16[32,14,3584]{2,1,0:T(8,128)(2,1)}), bf16[32,14,3584]{2,1,0:T(8,128)(2,1)}, u32[]{:S(2)}, u32[]{:S(2)}) async-start(bf16[32,14,3584]{2,1,0:T(8,128)(2,1)} %reshape.179), calls=%async_computation.2 | async-start | bytes 7340032 | tf_op jit(solution)/shard_map/all_to_all | solution.py:118
  132.8 8.2 %copy-start.8 = (f32[448,1024]{1,0:T(8,128)S(1)}, f32[448,1024]{1,0:T(8,128)}, u32[]{:S(2)}) copy-start(f32[448,1024]{1,0:T(8,128)} %fusion.12) | copy-start | bytes 5505028
  139.7 1.3 copy-start.9
  172.0 5.0 %copy-start.5 = (s32[1,128,2]{1,2,0:T(2,128)S(1)}, s32[1,128,2]{1,2,0:T(2,128)}, u32[]{:S(2)}) copy-start(s32[1,128,2]{1,2,0:T(2,128)} %param.12) | copy-start | bytes 3076
  172.0 52.6 %all-to-all-start.4 = ((bf16[32,14,3584]{2,1,0:T(8,128)(2,1)}), bf16[32,14,3584]{2,1,0:T(8,128)(2,1)}, u32[]{:S(2)}, u32[]{:S(2)}) async-start(bf16[32,14,3584]{2,1,0:T(8,128)(2,1)} %reshape.183), calls=%async_computation.4 | async-start | bytes 7340032 | tf_op jit(solution)/shard_map/all_to_all | solution.py:127
  236.0 6.5 %copy-start = (bf16[1,128,3584]{2,1,0:T(8,128)(2,1)S(1)}, bf16[1,128,3584]{2,1,0:T(8,128)(2,1)}, u32[]{:S(2)}) copy-start(bf16[1,128,3584]{2,1,0:T(8,128)(2,1)} %param.14) | copy-start | bytes 2752516
  242.5 1.2 copy-start.1
  242.5 1.4 copy-start.4
  334.5 5.0 %copy-start.7 = (f32[1,128,2]{1,2,0:T(2,128)S(1)}, f32[1,128,2]{1,2,0:T(2,128)}, u32[]{:S(2)}) copy-start(f32[1,128,2]{1,2,0:T(2,128)} %param.13) | copy-start | bytes 3076
  334.5 52.6 %all-to-all-start.1 = ((bf16[32,14,3584]{2,1,0:T(8,128)(2,1)}), bf16[32,14,3584]{2,1,0:T(8,128)(2,1)}, u32[]{:S(2)}, u32[]{:S(2)}) async-start(bf16[32,14,3584]{2,1,0:T(8,128)(2,1)} %reshape.176), calls=%async_computation.1 | async-start | bytes 7340032 | tf_op jit(solution)/shard_map/all_to_all | solution.py:109
  339.6 68.1 %collective-permute-start.1 = (bf16[128,3584]{1,0:T(8,128)(2,1)}, bf16[128,3584]{1,0:T(8,128)(2,1)}, u32[]{:S(2)}, u32[]{:S(2)}) collective-permute-start(bf16[128,3584]{1,0:T(8,128)(2,1)} %get-tuple-element.2), channel_id=1, source_target_pairs={{0,96},{32,0},{64,32},{96,64},{1,97},{33,1},{65,33},{97,65},{2,98}... | collective-permute-start | bytes 2752520 | tf_op jit(solution)/shard_map/ppermute | solution.py:11
  398.5 7.4 %copy-start.2 = (bf16[1,128,3584]{2,1,0:T(8,128)(2,1)S(1)}, bf16[1,128,3584]{2,1,0:T(8,128)(2,1)}, u32[]{:S(2)}) copy-start(bf16[1,128,3584]{2,1,0:T(8,128)(2,1)} %param.11) | copy-start | bytes 2752516
  406.0 21.3 %collective-permute-start = (bf16[128,3584]{1,0:T(8,128)(2,1)S(1)}, bf16[128,3584]{1,0:T(8,128)(2,1)S(1)}, u32[]{:S(2)}, u32[]{:S(2)}) collective-permute-start(bf16[128,3584]{1,0:T(8,128)(2,1)S(1)} %fusion.24), channel_id=1, source_target_pairs={{0,32},{32,64},{64,96},{96,0},{1,33},{33,65},{65,97},{97,1},{2,34}... | collective-permute-start | bytes 2752520 | tf_op jit(solution)/shard_map/ppermute | solution.py:11
where the time goes:
time: 439 us; the launch traced here: 431 us
  waiting for transfers between devices  173 us (39%)
  local copies, waits for them, and re-layouts  89.4 us (20%)
  matrix products  61.7 us (14%)
  blocking collectives  50.5 us (12%)
  starting transfers between devices  28.7 us (7%)
  other arithmetic  26.2 us (6%)
    all_to_all x1, blocking collectives, local(): lax.all_to_all(forward_send, 'expert', split_axis=0, concat_axis=0, tiled...  50.5 us
    all_to_all x1, waiting for transfers between devices, local(): lax.all_to_all(backward_out.reshape(groups, capacity, features), 'expert'...  44.4 us
    all_to_all x1, waiting for transfers between devices, local(): lax.all_to_all(forward_out.reshape(groups, capacity, features), 'expert',...  44.2 us
    all_to_all x1, waiting for transfers between devices, local(): lax.all_to_all(grad_send, 'expert', split_axis=0, concat_axis=0, tiled=True)  37.5 us
    all_to_all x1, waiting for transfers between devices, local(): lax.all_to_all(stored_send, 'expert', split_axis=0, concat_axis=0, tiled=...  27.1 us
    ppermute x2, waiting for transfers between devices, passed_along(): lax.ppermute(array, axis, [(i, (i + by) % devices) for i in range(devices)])  19.6 us
    dot_general x1, matrix products, expert_backward(): jnp.einsum('mf,df->md', gate_grad, gate_matrix, preferred_element_type=jn...  16.9 us
    dot_general x1, matrix products, expert_forward(): jnp.dot(active, down_matrix, preferred_element_type=jnp.float32)  14.3 us
  transfers between devices with their start and end apart: 6, of which 5 were waited for; matrix products, arithmetic and copies ran while one was open for 12% of the time, Pallas kernels for 0%

commit v1 on v0

v1 whole, which is shorter than its diff:
```python
import functools

import jax
import jax.numpy as jnp
from jax import lax
from jax.experimental import pallas as pl
from jax.experimental.pallas import tpu as pltpu
from jax.sharding import PartitionSpec as P

EPSILON = 1e-06
MESH = pl.DeviceIdType.MESH
BF = jnp.bfloat16
F32 = jnp.float32
D = 3584
FE = 1024
HALF = D // 2
QUARTER = D // 4
SIDE = 4
SLOTS = 14
CHUNKS = ((0, 512), (512, 384))
STEP = 256


def dot(a, b):
    return jnp.dot(a, b, preferred_element_type=F32)


def dot_nt(a, b):
    return lax.dot_general(a, b, (((1,), (1,)), ((), ())), preferred_element_type=F32)


def rows(value):
    return value.reshape(value.shape[-3] * value.shape[-2], value.shape[-1])


def tiles(value):
    return value.reshape(value.shape[0] // 16, 16, value.shape[1])


def split(value):
    high = value.astype(BF)
    return high, (value - high.astype(F32)).astype(BF)


def kernel(
    rg, fin, bin_, upg, gain, wg, wu, wd, fo, bo,
    WG, WU, WD, G, XA, YB, S, L, OWN, RG, PA, PB, GG, UG, PERM, TRI, EYE,
    s_rg_r, s_rg_s, s_g_r, s_g_s, s_x_r, s_x_s, s_r_r, s_r_s,
    s_t1_r, s_t1_s, s_t2_r, s_t2_s, s_c_r, s_y_r, s_y_s, s_w, s_o, s_l,
):
    pipe = lax.axis_index("pipe")
    me = lax.axis_index("expert")
    core = lax.rem(me, 2)
    other = 1 - core
    ring = (lax.rem(me // 2, SIDE), me // (2 * SIDE))
    X = (XA, YB)

    def at(h, delta):
        return lax.rem(ring[h] + delta, SIDE)

    def dev(h, delta, k):
        r = at(h, delta)
        if h == 0:
            return (pipe, (ring[1] * SIDE + r) * 2 + k)
        return (pipe, (r * SIDE + ring[0]) * 2 + k)

    def cols(h, q, c0=0, cw=QUARTER):
        return pl.ds(pl.multiple_of(h * HALF + q * QUARTER + c0, 128), cw)

    def qcols(q, c0=0, cw=QUARTER):
        return pl.ds(pl.multiple_of(q * QUARTER + c0, 128), cw)

    def send(src, dst, ss, rs, device):
        pltpu.make_async_remote_copy(
            src_ref=src, dst_ref=dst, send_sem=ss, recv_sem=rs, device_id=device, device_id_type=MESH
        ).start()

    def copy(src, dst, sem):
        pltpu.make_async_copy(src, dst, sem).start()

    def wait(ref, sem):
        pltpu.make_async_copy(ref, ref, sem).wait()

    copy(upg, OWN.at[0], s_o.at[0])
    copy(bin_, OWN.at[1], s_o.at[1])
    copy(fin, OWN.at[2], s_o.at[2])

    barrier = pltpu.get_barrier_semaphore()
    peers = [dev(h, d, k) for h in (0, 1) for d in (1, 2, 3) for k in (0, 1)]
    peers.append(dev(0, 0, other))
    ahead = (lax.rem(pipe + 1, SIDE), me)
    behind = (lax.rem(pipe + 3, SIDE), me)
    peers += [ahead, behind]
    for peer in peers:
        pl.semaphore_signal(barrier, inc=1, device_id=peer, device_id_type=MESH)
    pl.semaphore_wait(barrier, len(peers))

    for h in (0, 1):
        mine = ring[h] * 2 + core
        for d in (1, 2, 3):
            for k in (0, 1):
                send(rg, RG.at[h, mine], s_rg_s.at[h], s_rg_r.at[h], dev(h, d, k))
        send(rg, RG.at[h, mine], s_rg_s.at[h], s_rg_r.at[h], dev(h, 0, other))
        copy(rg, RG.at[h, mine], s_rg_r.at[h])

    def gather_start(a):
        for h in (0, 1):
            mine = ring[h] * 2 + core
            for d, k in ((1, 0), (3, 1)):
                for q in (0, 1):
                    send(OWN.at[a, :, :, cols(h, q)], G.at[a, h, mine], s_g_s.at[a, h], s_g_r.at[a, h, k], dev(h, d, q))
            send(OWN.at[a, :, :, cols(h, other)], G.at[a, h, mine], s_g_s.at[a, h], s_g_r.at[a, h, 4], dev(h, 0, other))
            copy(OWN.at[a, :, :, cols(h, core)], G.at[a, h, mine], s_g_r.at[a, h, 5])

    def gather_forward(a):
        for h in (0, 1):
            left = 2 * at(h, 3)
            wait(G.at[a, h, pl.ds(left, 2)], s_g_r.at[a, h, 0])
            for k in (0, 1):
                part = G.at[a, h, left + k, pl.ds(0, 4)]
                send(part, part, s_g_s.at[a, h], s_g_r.at[a, h, 2], dev(h, 1, core))
        for h in (0, 1):
            right = 2 * at(h, 1)
            wait(G.at[a, h, pl.ds(right, 2)], s_g_r.at[a, h, 1])
            for k in (0, 1):
                part = G.at[a, h, right + k, pl.ds(4, 4)]
                send(part, part, s_g_s.at[a, h], s_g_r.at[a, h, 3], dev(h, 3, core))

    def gather_finish(a, h):
        far = 2 * at(h, 2)
        wait(G.at[a, h, pl.ds(far, 2), pl.ds(0, 4)], s_g_r.at[a, h, 2])
        wait(G.at[a, h, pl.ds(far, 2), pl.ds(4, 4)], s_g_r.at[a, h, 3])
        wait(G.at[a, h, ring[h] * 2 + other], s_g_r.at[a, h, 4])
        wait(G.at[a, h, ring[h] * 2 + core], s_g_r.at[a, h, 5])

    def gather_sent(a):
        for h in (0, 1):
            wait(G.at[a, h, pl.ds(0, 7)], s_g_s.at[a, h])

    def normalize(a):
        def body(k, carry):
            v = OWN[a, k].astype(F32)
            r = lax.rsqrt(jnp.mean(v * v, axis=-1, keepdims=True) + EPSILON)
            OWN[a, k] = (v * r * gain[...]).astype(BF)
            return carry

        lax.fori_loop(0, 8, body, 0)

    wait(OWN.at[0], s_o.at[0])
    gather_start(0)
    wait(OWN.at[1], s_o.at[1])
    normalize(1)
    gather_start(1)
    copy(wg, WG, s_w.at[0])
    copy(wu, WU, s_w.at[1])
    copy(wd, WD, s_w.at[2])
    wait(OWN.at[2], s_o.at[2])
    normalize(2)

    up = lax.broadcasted_iota(jnp.int32, (128, 128), 0)
    across = lax.broadcasted_iota(jnp.int32, (128, 128), 1)
    TRI[...] = jnp.where(up < across, 1.0, 0.0).astype(BF)
    EYE[...] = jnp.where(up == across, 1.0, 0.0).astype(BF)
    line = lax.broadcasted_iota(jnp.int32, (448, 448), 0)
    outer = (line >= 112).astype(jnp.int32) + (line >= 224).astype(jnp.int32) + (line >= 336).astype(jnp.int32)
    rest = line - 112 * outer
    inner = (rest >= 28).astype(jnp.int32) + (rest >= 56).astype(jnp.int32) + (rest >= 84).astype(jnp.int32)
    place = 112 * inner + 28 * outer + rest - 28 * inner
    PERM[...] = jnp.where(lax.broadcasted_iota(jnp.int32, (448, 448), 1) == place, 1.0, 0.0).astype(BF)

    def experts(h):
        e = up // 16
        if h == 0:
            ids = (e // 2) * (2 * SIDE) + ring[0] * 2 + e % 2
        else:
            ids = ring[1] * (2 * SIDE) + e
        return ids.astype(F32)

    ids = [experts(h) for h in (0, 1)]
    in_tile = (up % 16).astype(F32)

    def route_row(h, s, row):
        return RG[h, s, pl.ds(row, 1), :]

    def build(st, h):
        def body(s, carry):
            named = (route_row(h, s, 4 * st) == ids[h]) | (route_row(h, s, 4 * st + 1) == ids[h])
            mask = jnp.where(named, 1.0, 0.0)
            before = dot(mask.astype(BF), TRI[...])
            first = 2.0 * s.astype(F32) + in_tile
            PA[st, h, s] = jnp.where(before == first, mask, 0.0).astype(BF)
            PB[st, h, s] = jnp.where(before == first - 16.0, mask, 0.0).astype(BF)
            return carry

        lax.fori_loop(0, 8, body, 0)

    def gates(st, h, s):
        return jnp.where(route_row(h, s, 4 * st) == ids[h], route_row(h, s, 4 * st + 2), route_row(h, s, 4 * st + 3))

    for h in (0, 1):
        wait(RG.at[h], s_rg_r.at[h])
    for st in (1, 0):
        for h in (0, 1):
            build(st, h)

    def pack(a, st, h, b, gated):
        def body(i, carry):
            both = rows(G[a, h, pl.ds(i, 2)].reshape(16, 16, QUARTER))
            pick = jnp.concatenate([PA[st, h, i], PB[st, h, i + 1]], axis=1)
            if gated:
                weight = jnp.concatenate([gates(st, h, i), gates(st, h, i + 1)], axis=1)
                high, low = split(pick.astype(F32) * weight)
                out = dot(high, both) + dot(low, both)
            else:
                out = dot(pick, both)
            S[b, h, :, i] = tiles(out.astype(BF))
            return carry

        lax.fori_loop(0, 7, body, 0)

    def scatter_start(a, h, b):
        place_at = pl.ds(7 * ring[1 - h], 7)
        for d in (1, 3, 2):
            for k in (0, 1):
                send(
                    S.at[b, h, 2 * at(1 - h, d) + k, pl.ds(0, 7)], X[h].at[a, place_at, :, qcols(core)],
                    s_x_s.at[a, h], s_x_r.at[a, h], dev(1 - h, d, k),
                )
        send(
            S.at[b, h, 2 * ring[1 - h] + other, pl.ds(0, 7)], X[h].at[a, place_at, :, qcols(core)],
            s_x_s.at[a, h], s_x_r.at[a, h], dev(1 - h, 0, other),
        )
        copy(S.at[b, h, 2 * ring[1 - h] + core, pl.ds(0, 7)], X[h].at[a, place_at, :, qcols(core)], s_l.at[a, h])

    def scatter_sent(a, b):
        for h in (0, 1):
            wait(S.at[b, h, pl.ds(0, 7), pl.ds(0, 7)], s_x_s.at[a, h])
            wait(S.at[b, h, 0, pl.ds(0, 7)], s_l.at[a, h])

    def scatter_finish(a, b):
        for h in (0, 1):
            wait(S.at[b, h, pl.ds(0, 7), pl.ds(0, 7)], s_x_r.at[a, h])

    gather_forward(0)
    for h in (0, 1):
        gather_finish(0, h)
        pack(0, 1, h, 0, True)
        scatter_start(0, h, 0)
    gather_start(2)
    gather_forward(1)
    gather_sent(0)
    for h in (0, 1):
        gather_finish(1, h)
        pack(1, 1, h, 1, False)
        scatter_start(1, h, 1)
    gather_forward(2)
    gather_sent(1)
    scatter_sent(0, 0)
    for h in (0, 1):
        gather_finish(2, h)
        pack(2, 0, h, 0, False)
    gather_sent(2)
    for h in (0, 1):
        scatter_start(2, h, 0)

    def exchange(a):
        def body(n, carry):
            at_cols = pl.ds(pl.multiple_of(n * STEP, STEP), STEP)
            YB[a, :, :, at_cols] = tiles(dot(PERM[...], rows(YB[a, :, :, at_cols])).astype(BF))
            return carry

        lax.fori_loop(0, HALF // STEP, body, 0)

    def exchange_hidden(src, dst):
        def body(n, carry):
            at_cols = pl.ds(pl.multiple_of(n * STEP, STEP), STEP)
            dst[1, :, :, at_cols] = tiles(dot(PERM[...], src[:, at_cols]).astype(BF))
            return carry

        lax.fori_loop(0, FE // STEP, body, 0)

    scatter_finish(0, 0)
    exchange(0)
    wait(WG, s_w.at[0])
    wait(WU, s_w.at[1])
    wait(WD, s_w.at[2])
    scatter_finish(1, 1)
    scatter_sent(1, 1)
    exchange(1)

    def into(a, W, at_cols):
        return dot(rows(XA[a]), W[pl.ds(0, HALF), at_cols]) + dot(rows(YB[a]), W[pl.ds(HALF, HALF), at_cols])

    def backward_hidden(f, carry):
        at_cols = pl.ds(pl.multiple_of(f * STEP, STEP), STEP)
        pre_gate = into(1, WG, at_cols)
        pre_up = into(1, WU, at_cols)
        hidden = dot_nt(rows(XA[0]), WD[at_cols, pl.ds(0, HALF)]) + dot_nt(rows(YB[0]), WD[at_cols, pl.ds(HALF, HALF)])
        sig = 1.0 / (1.0 + jnp.exp(-pre_gate))
        GG[:, at_cols] = (hidden * pre_up * sig * (1.0 + pre_gate * (1.0 - sig))).astype(BF)
        UG[:, at_cols] = (hidden * pre_gate * sig).astype(BF)
        return carry

    lax.fori_loop(0, FE // STEP, backward_hidden, 0)
    exchange_hidden(GG, XA)
    exchange_hidden(UG, YB)

    def return_start(b, ch, h, a):
        c0, cw = ((0, QUARTER),) [0] if b == 0 else CHUNKS[ch]
        gb = b
        mine = 2 * ring[1 - h] + core
        n = b * len(CHUNKS) + ch
        dst = G.at[gb, h, pl.ds(0, 7), mine, :, pl.ds(c0, cw)]
        for d in (1, 3, 2):
            for q in (0, 1):
                send(
                    X[h].at[a, pl.ds(7 * at(1 - h, d), 7), :, qcols(q, c0, cw)], dst,
                    s_r_s.at[n, h], s_r_r.at[n, h], dev(1 - h, d, q),
                )
        home = pl.ds(7 * ring[1 - h], 7)
        send(X[h].at[a, home, :, qcols(other, c0, cw)], dst, s_r_s.at[n, h], s_r_r.at[n, h], dev(1 - h, 0, other))
        copy(X[h].at[a, home, :, qcols(core, c0, cw)], dst, s_r_r.at[n, h])

    for h in (0, 1):

        def backward_out(n, carry):
            at_rows = pl.ds(pl.multiple_of(h * HALF + n * STEP, STEP), STEP)
            at_cols = pl.ds(pl.multiple_of(n * STEP, STEP), STEP)
            if h == 0:
                gg, ug = GG[...], UG[...]
            else:
                gg, ug = rows(XA[1, :, :, pl.ds(0, FE)]), rows(YB[1, :, :, pl.ds(0, FE)])
            X[h][0, :, :, at_cols] = tiles((dot_nt(gg, WG[at_rows, :]) + dot_nt(ug, WU[at_rows, :])).astype(BF))
            return carry

        lax.fori_loop(0, HALF // STEP, backward_out, 0)
        return_start(0, 0, h, 0)

    scatter_finish(2, 0)
    scatter_sent(2, 0)
    exchange(2)

    def forward_hidden(f, carry):
        at_cols = pl.ds(pl.multiple_of(f * STEP, STEP), STEP)
        pre_gate = into(2, WG, at_cols)
        pre_up = into(2, WU, at_cols)
        GG[:, at_cols] = (pre_gate * pre_up / (1.0 + jnp.exp(-pre_gate))).astype(BF)
        return carry

    lax.fori_loop(0, FE // STEP, forward_hidden, 0)
    exchange_hidden(GG, XA)
    for ch, (c0, cw) in enumerate(CHUNKS):
        for h in (0, 1):
            for q in (0, 1):
                for n in range(0, cw, STEP):
                    w = min(STEP, cw - n)
                    act = GG[...] if h == 0 else rows(XA[1, :, :, pl.ds(0, FE)])
                    start = q * QUARTER + c0 + n
                    X[h][2, :, :, pl.ds(start, w)] = tiles(dot(act, WD[:, pl.ds(h * HALF + start, w)]).astype(BF))
            return_start(1, ch, h, 2)

    copy(bin_, OWN.at[1], s_o.at[1])
    copy(fin, OWN.at[2], s_o.at[2])

    def combine(b, ch, h):
        c0, cw = (0, QUARTER) if b == 0 else CHUNKS[ch]
        st, to = (1, 1) if b == 0 else (0, 0)
        here = pl.ds(c0, cw)

        def body(s, carry):
            prev = rows(G[b, h, jnp.maximum(s - 1, 0), :, :, here])
            cur = rows(G[b, h, jnp.minimum(s, 6), :, :, here])
            pa, pb = PA[st, h, s], PB[st, h, s]
            if b == 0:
                out = dot(dot_nt(EYE[...], pb).astype(BF), prev) + dot(dot_nt(EYE[...], pa).astype(BF), cur)
            else:
                weight = gates(st, h, s)
                out = 0.0
                for pick, block in ((pb, prev), (pa, cur)):
                    for part in split(pick.astype(F32) * weight):
                        out = out + dot(dot_nt(EYE[...], part).astype(BF), block)
            S[to, h, s, :, :, here] = tiles(out.astype(BF))
            return carry

        lax.fori_loop(0, 8, body, 0)

    def land(b):
        return L if b == 0 else G.at[2]

    def meta(b, ch):
        c0, cw = (0, QUARTER) if b == 0 else CHUNKS[ch]
        return b * len(CHUNKS) + ch, pl.ds(c0, cw), (1 if b == 0 else 0), land(b)

    def far_start(b, ch, h):
        n, here, to, B = meta(b, ch)
        far = 2 * at(h, 2)
        for k in (0, 1):
            send(S.at[to, h, far + k, pl.ds(0, 4), :, here], B.at[h, 6, pl.ds(4 * k, 4), :, here], s_t1_s.at[n, h], s_t1_r.at[n, h, 0], dev(h, 1, core))
            send(S.at[to, h, far + k, pl.ds(4, 4), :, here], B.at[h, 7, pl.ds(4 * k, 4), :, here], s_t1_s.at[n, h], s_t1_r.at[n, h, 1], dev(h, 3, core))
        send(S.at[to, h, 2 * ring[h] + other, :, :, here], B.at[h, 4 + core, :, :, here], s_t2_s.at[n, h], s_c_r.at[n, h, 0], dev(h, 0, other))
        copy(S.at[to, h, 2 * ring[h] + core, :, :, here], B.at[h, 4 + core, :, :, here], s_c_r.at[n, h, 1])

    def near_start(b, ch, h):
        n, here, to, B = meta(b, ch)
        for slot, d, t0, base in ((6, 1, 0, 0), (7, 3, 4, 2)):
            wait(B.at[h, slot, :, :, here], s_t1_r.at[n, h, slot - 6])
            near = 2 * at(h, d)
            for k in (0, 1):
                own = S[to, h, near + k, pl.ds(t0, 4), :, here].astype(F32)
                got = B[h, slot, pl.ds(4 * k, 4), :, here].astype(F32)
                S[to, h, near + k, pl.ds(t0, 4), :, here] = (own + got).astype(BF)
                send(S.at[to, h, near + k, :, :, here], B.at[h, base + core, :, :, here], s_t2_s.at[n, h], s_t2_r.at[n, h], dev(h, d, k))

    def near_finish(b, ch, h):
        n, here, to, B = meta(b, ch)
        wait(B.at[h, pl.ds(0, 4), :, :, here], s_t2_r.at[n, h])
        wait(B.at[h, 4 + other, :, :, here], s_c_r.at[n, h, 0])
        wait(B.at[h, 4 + core, :, :, here], s_c_r.at[n, h, 1])

    def arrived(b, h, q, k, here):
        B = land(b)
        return B[h, q, k, :, here].astype(F32) + B[h, 2 + q, k, :, here].astype(F32) + B[h, 4 + q, k, :, here].astype(F32)

    for h in (0, 1):
        wait(G.at[0, h, pl.ds(0, 7)], s_r_r.at[0, h])
        combine(0, 0, h)
        far_start(0, 0, h)
    for h in (0, 1):
        near_start(0, 0, h)

    def forward_relay(ch):
        n, here, to, B = meta(1, ch)
        for h in (0, 1):
            wait(G.at[1, h, pl.ds(0, 7), :, :, here], s_r_r.at[n, h])
            combine(1, ch, h)
            far_start(1, ch, h)
        for h in (0, 1):
            near_start(1, ch, h)

    forward_relay(0)

    for h in (0, 1):
        near_finish(0, 0, h)
    wait(OWN.at[1], s_o.at[1])
    wait(OWN.at[2], s_o.at[2])

    def backward_last(k, carry):
        summed = jnp.concatenate([arrived(0, h, q, k, pl.ds(0, QUARTER)) for h in (0, 1) for q in (0, 1)], axis=1)
        stored = OWN[1, k].astype(F32)
        r = lax.rsqrt(jnp.mean(stored * stored, axis=-1, keepdims=True) + EPSILON)
        grad = gain[...] * summed
        mean = jnp.mean(stored * grad, axis=-1, keepdims=True)
        OWN[1, k] = (OWN[0, k].astype(F32) + r * grad - stored * (r * r * r) * mean).astype(BF)
        return carry

    lax.fori_loop(0, 8, backward_last, 0)
    send(OWN.at[1], bo, s_y_s.at[0], s_y_r.at[0], behind)

    def forward_last(ch):
        c0, cw = CHUNKS[ch]
        n, here, to, B = meta(1, ch)
        for h in (0, 1):
            near_finish(1, ch, h)

            def body(k, carry):
                for q in (0, 1):
                    spot = pl.ds(h * HALF + q * QUARTER + c0, cw)
                    OWN[2, k, :, spot] = (OWN[2, k, :, spot].astype(F32) + arrived(1, h, q, k, here)).astype(BF)
                return carry

            lax.fori_loop(0, 8, body, 0)
            for q in (0, 1):
                spot = pl.ds(h * HALF + q * QUARTER + c0, cw)
                send(OWN.at[2, :, :, spot], fo.at[:, :, spot], s_y_s.at[1 + ch], s_y_r.at[1 + ch], ahead)

    for ch in range(1, len(CHUNKS)):
        forward_relay(ch)
        forward_last(ch - 1)
    forward_last(len(CHUNKS) - 1)

    for h in (0, 1):
        wait(RG.at[h, pl.ds(0, 7)], s_rg_s.at[h])
    for b, chunks in ((0, ((0, QUARTER),)), (1, CHUNKS)):
        for ch, (c0, cw) in enumerate(chunks):
            n, here, to, B = meta(b, ch)
            for h in (0, 1):
                wait(S.at[to, h, pl.ds(0, 7), pl.ds(0, 7), :, here], s_r_s.at[n, h])
                wait(S.at[to, h, pl.ds(0, 2), :, :, here], s_t1_s.at[n, h])
                wait(S.at[to, h, pl.ds(0, 5), :, :, here], s_t2_s.at[n, h])
    wait(bo, s_y_s.at[0])
    wait(bo, s_y_r.at[0])
    for ch, (c0, cw) in enumerate(CHUNKS):
        wait(fo.at[:, :, pl.ds(0, 4 * cw)], s_y_s.at[1 + ch])
        wait(fo.at[:, :, pl.ds(0, 4 * cw)], s_y_r.at[1 + ch])


def local(
    forward_input,
    forward_routes,
    forward_gates,
    backward_input,
    backward_routes,
    backward_gates,
    upstream_gradient,
    norm_gain,
    gate_weight,
    up_weight,
    down_weight,
):
    rg = jnp.concatenate(
        [forward_routes[0].astype(F32), forward_gates[0], backward_routes[0].astype(F32), backward_gates[0]], axis=1
    ).T
    shape = (8, 16, D)
    parts = 1 + len(CHUNKS)
    groups = 2 * len(CHUNKS)
    dma = pltpu.SemaphoreType.DMA
    vmem = pl.BlockSpec(memory_space=pltpu.VMEM)
    anywhere = pl.BlockSpec(memory_space=pl.ANY)
    fo, bo = pl.pallas_call(
        kernel,
        name="relay",
        out_shape=(jax.ShapeDtypeStruct(shape, BF), jax.ShapeDtypeStruct(shape, BF)),
        in_specs=[vmem, anywhere, anywhere, anywhere, vmem, anywhere, anywhere, anywhere],
        out_specs=(anywhere, anywhere),
        scratch_shapes=[
            pltpu.VMEM((D, FE), BF),
            pltpu.VMEM((D, FE), BF),
            pltpu.VMEM((FE, D), BF),
            pltpu.VMEM((3, 2, 8, 8, 16, QUARTER), BF),
            pltpu.VMEM((3, 28, 16, HALF), BF),
            pltpu.VMEM((3, 28, 16, HALF), BF),
            pltpu.VMEM((2, 2, 8, 8, 16, QUARTER), BF),
            pltpu.VMEM((2, 8, 8, 16, QUARTER), BF),
            pltpu.VMEM((3, 8, 16, D), BF),
            pltpu.VMEM((2, 8, 8, 128), F32),
            pltpu.VMEM((2, 2, 8, 128, 128), BF),
            pltpu.VMEM((2, 2, 8, 128, 128), BF),
            pltpu.VMEM((448, FE), BF),
            pltpu.VMEM((448, FE), BF),
            pltpu.VMEM((448, 448), BF),
            pltpu.VMEM((128, 128), BF),
            pltpu.VMEM((128, 128), BF),
            dma((2,)),
            dma((2,)),
            dma((3, 2, 6)),
            dma((3, 2)),
            dma((3, 2)),
            dma((3, 2)),
            dma((groups, 2)),
            dma((groups, 2)),
            dma((groups, 2, 2)),
            dma((groups, 2)),
            dma((groups, 2)),
            dma((groups, 2)),
            dma((groups, 2, 2)),
            dma((parts,)),
            dma((parts,)),
            dma((3,)),
            dma((3,)),
            dma((3, 2)),
        ],
        compiler_params=pltpu.CompilerParams(
            collective_id=0, has_side_effects=True, vmem_limit_bytes=64 * 1024 * 1024 - 65536
        ),
        cost_estimate=pl.CostEstimate(flops=46 * 10**9, bytes_accessed=30 * 10**6, transcendentals=10**6),
    )(
        rg,
        forward_input.reshape(shape),
        backward_input.reshape(shape),
        upstream_gradient.reshape(shape),
        norm_gain.astype(F32),
        gate_weight[0, 0],
        up_weight[0, 0],
        down_weight[0, 0],
    )
    return (fo.reshape(1, 128, D), bo.reshape(1, 128, D))


def solution(mesh):
    rows_spec = P("pipe", "expert", None)
    weight = P("pipe", "expert", None, None)
    in_specs = (rows_spec,) * 7 + (P("pipe", None), weight, weight, weight)
    out_specs = (rows_spec, rows_spec)
    return jax.shard_map(local, mesh=mesh, in_specs=in_specs, out_specs=out_specs, check_vma=False)
```

time: 439 us -> 236 us (0.54); the launches traced: 431 us -> 235 us
  Pallas kernels: 0 us -> 227 us
  waiting for transfers between devices: 173 us -> 0 us
  local copies, waits for them, and re-layouts: 89.4 us -> 4.32 us
  matrix products: 61.7 us -> 0 us
  blocking collectives: 50.5 us -> 0 us
  starting transfers between devices: 28.7 us -> 0 us
  other arithmetic: 26.2 us -> 3.32 us
    pallas_call x0 -> x1, Pallas kernels: none -> 227 us  [local(): pl.pallas_call(kernel, name='relay', out_shape=(jax.ShapeDtypeStruct(shap...]
    all_to_all x4 -> x0, waiting for transfers between devices: 153 us -> none  [the longest x1 44.4 us: local(): lax.all_to_all(backward_out.reshape(groups, capacity, features), 'expert'...]
    dot_general x6 -> x0, matrix products: 61.7 us -> none  [the longest x1 16.9 us: expert_backward(): jnp.einsum('mf,df->md', gate_grad, gate_matrix, preferred_element_type=jn...]
    all_to_all x1 -> x0, blocking collectives: 50.5 us -> none  [local(): lax.all_to_all(forward_send, 'expert', split_axis=0, concat_axis=0, tiled...]
    reshape x10 -> x0, local copies, waits for them, and re-layouts: 40.8 us -> none  [the longest x3 14 us: pack_rows(): return padded[source].reshape(groups, capacity, block.shape[1])]
    all_to_all x4 -> x0, starting transfers between devices: 23.7 us -> none  [the longest x1 8.49 us: local(): lax.all_to_all(stored_send, 'expert', split_axis=0, concat_axis=0, tiled=...]
    ppermute x2 -> x0, waiting for transfers between devices: 19.6 us -> none  [passed_along(): lax.ppermute(array, axis, [(i, (i + by) % devices) for i in range(devices)])]
    gather x5 -> x0, local copies, waits for them, and re-layouts: 18.1 us -> none  [the longest x3 12.1 us: pack_rows(): return padded[source].reshape(groups, capacity, block.shape[1])]
  transfers between devices with their start and end apart: 6 -> 0, of which waited for: 5 -> 0; matrix products, arithmetic and copies ran while one was open for 12% -> 0% of each run, Pallas kernels for 0% -> 0%
where the time goes in v1:
time: 236 us; the launch traced here: 235 us
  Pallas kernels  227 us (96%)
  local copies, waits for them, and re-layouts  4.32 us (2%)
  other arithmetic  3.32 us (1%)
    pallas_call x1, Pallas kernels, local(): pl.pallas_call(kernel, name='relay', out_shape=(jax.ShapeDtypeStruct(shap...  227 us

profile of v1, /device:TPU:0, one launch (start us, length us, event | category | flops | bytes accessed | tf_op | source)
XLA Modules:
  0.0 235.3 jit_solution(4697946340092034296)
XLA Ops:
  0.6 0.7 convert_bitcast_fusion
  1.3 1.3 maximum_bitcast_fusion.rg
  2.6 1.3 convert_element_type.19.gain
  4.0 227.0 %relay.1 = (bf16[8,16,3584]{2,1,0:T(8,128)(2,1)}, bf16[8,16,3584]{2,1,0:T(8,128)(2,1)}) custom-call(f32[8,128]{1,0:T(8,128)} %maximum_bitcast_fusion.rg, bf16[8,16,3584]{2,1,0:T(8,128)(2,1)} %bitcast.23, bf16[8,16,3584]{2,1,0:T(8,128)(2,1)} %bitcast.24, bf16[8,16,3584]{2,1,0:T(8,128)(2,1)} %bitcast.25, f32[1,3584]{1,0:T(1,128)} %convert_element_type.19.gain, ...), custom_call_target="tpu_custom_call" | custom-call | flops 46000001024 | bytes 30000000 | tf_op jit(solution)/shard_map/relay/pallas_call | solution.py:519
  231.0 2.2 copy.15
  233.2 2.2 copy.16

commit v2 on v1

--- a/solution.py
+++ b/solution.py
@@ -17,7 +17,7 @@
 QUARTER = D // 4
 SIDE = 4
 SLOTS = 14
-CHUNKS = ((0, 512), (512, 384))
+CHUNKS = ((0, 512), (512, 256), (768, 128))
 STEP = 256
 
 
@@ -43,8 +43,8 @@
 
 
 def kernel(
-    rg, fin, bin_, upg, gain, wg, wu, wd, fo, bo,
-    WG, WU, WD, G, XA, YB, S, L, OWN, RG, PA, PB, GG, UG, PERM, TRI, EYE,
+    fr, fg, br, bg, fin, bin_, upg, gain, wg, wu, wd, fo, bo,
+    WG, WU, WD, G, XA, YB, S, L, OWN, RG, PA, PB, GG, UG, HID, PERM, TRI, EYE, PT, PG, rg,
     s_rg_r, s_rg_s, s_g_r, s_g_s, s_x_r, s_x_s, s_r_r, s_r_s,
     s_t1_r, s_t1_s, s_t2_r, s_t2_s, s_c_r, s_y_r, s_y_s, s_w, s_o, s_l,
 ):
@@ -85,6 +85,11 @@
     copy(bin_, OWN.at[1], s_o.at[1])
     copy(fin, OWN.at[2], s_o.at[2])
 
+    rg[pl.ds(0, 2), :] = fr[...].astype(F32)
+    rg[pl.ds(2, 2), :] = fg[...]
+    rg[pl.ds(4, 2), :] = br[...].astype(F32)
+    rg[pl.ds(6, 2), :] = bg[...]
+
     barrier = pltpu.get_barrier_semaphore()
     peers = [dev(h, d, k) for h in (0, 1) for d in (1, 2, 3) for k in (0, 1)]
     peers.append(dev(0, 0, other))
@@ -93,70 +98,17 @@
     peers += [ahead, behind]
     for peer in peers:
         pl.semaphore_signal(barrier, inc=1, device_id=peer, device_id_type=MESH)
-    pl.semaphore_wait(barrier, len(peers))
-
-    for h in (0, 1):
-        mine = ring[h] * 2 + core
-        for d in (1, 2, 3):
-            for k in (0, 1):
-                send(rg, RG.at[h, mine], s_rg_s.at[h], s_rg_r.at[h], dev(h, d, k))
-        send(rg, RG.at[h, mine], s_rg_s.at[h], s_rg_r.at[h], dev(h, 0, other))
-        copy(rg, RG.at[h, mine], s_rg_r.at[h])
-
-    def gather_start(a):
-        for h in (0, 1):
-            mine = ring[h] * 2 + core
-            for d, k in ((1, 0), (3, 1)):
-                for q in (0, 1):
-                    send(OWN.at[a, :, :, cols(h, q)], G.at[a, h, mine], s_g_s.at[a, h], s_g_r.at[a, h, k], dev(h, d, q))
-            send(OWN.at[a, :, :, cols(h, other)], G.at[a, h, mine], s_g_s.at[a, h], s_g_r.at[a, h, 4], dev(h, 0, other))
-            copy(OWN.at[a, :, :, cols(h, core)], G.at[a, h, mine], s_g_r.at[a, h, 5])
-
-    def gather_forward(a):
-        for h in (0, 1):
-            left = 2 * at(h, 3)
-            wait(G.at[a, h, pl.ds(left, 2)], s_g_r.at[a, h, 0])
-            for k in (0, 1):
-                part = G.at[a, h, left + k, pl.ds(0, 4)]
-                send(part, part, s_g_s.at[a, h], s_g_r.at[a, h, 2], dev(h, 1, core))
-        for h in (0, 1):
-            right = 2 * at(h, 1)
-            wait(G.at[a, h, pl.ds(right, 2)], s_g_r.at[a, h, 1])
-            for k in (0, 1):
-                part = G.at[a, h, right + k, pl.ds(4, 4)]
-                send(part, part, s_g_s.at[a, h], s_g_r.at[a, h, 3], dev(h, 3, core))
-
-    def gather_finish(a, h):
-        far = 2 * at(h, 2)
-        wait(G.at[a, h, pl.ds(far, 2), pl.ds(0, 4)], s_g_r.at[a, h, 2])
-        wait(G.at[a, h, pl.ds(far, 2), pl.ds(4, 4)], s_g_r.at[a, h, 3])
-        wait(G.at[a, h, ring[h] * 2 + other], s_g_r.at[a, h, 4])
-        wait(G.at[a, h, ring[h] * 2 + core], s_g_r.at[a, h, 5])
-
-    def gather_sent(a):
-        for h in (0, 1):
-            wait(G.at[a, h, pl.ds(0, 7)], s_g_s.at[a, h])
-
     def normalize(a):
         def body(k, carry):
             v = OWN[a, k].astype(F32)
             r = lax.rsqrt(jnp.mean(v * v, axis=-1, keepdims=True) + EPSILON)
-            OWN[a, k] = (v * r * gain[...]).astype(BF)
+            OWN[a, k] = (v * r * gain[...].astype(F32)).astype(BF)
             return carry
 
         lax.fori_loop(0, 8, body, 0)
 
-    wait(OWN.at[0], s_o.at[0])
-    gather_start(0)
     wait(OWN.at[1], s_o.at[1])
     normalize(1)
-    gather_start(1)
-    copy(wg, WG, s_w.at[0])
-    copy(wu, WU, s_w.at[1])
-    copy(wd, WD, s_w.at[2])
-    wait(OWN.at[2], s_o.at[2])
-    normalize(2)
-
     up = lax.broadcasted_iota(jnp.int32, (128, 128), 0)
     across = lax.broadcasted_iota(jnp.int32, (128, 128), 1)
     TRI[...] = jnp.where(up < across, 1.0, 0.0).astype(BF)
@@ -168,6 +120,58 @@
     place = 112 * inner + 28 * outer + rest - 28 * inner
     PERM[...] = jnp.where(lax.broadcasted_iota(jnp.int32, (448, 448), 1) == place, 1.0, 0.0).astype(BF)
 
+    pl.semaphore_wait(barrier, len(peers))
+
+    for h in (0, 1):
+        mine = ring[h] * 2 + core
+        for d in (1, 2, 3):
+            for k in (0, 1):
+                send(rg, RG.at[h, mine], s_rg_s.at[h], s_rg_r.at[h], dev(h, d, k))
+        send(rg, RG.at[h, mine], s_rg_s.at[h], s_rg_r.at[h], dev(h, 0, other))
+        copy(rg, RG.at[h, mine], s_rg_r.at[h])
+
+    def gather_start(a):
+        for h in (0, 1):
+            mine = ring[h] * 2 + core
+            for d, k in ((1, 0), (3, 1)):
+                for q in (0, 1):
+                    send(OWN.at[a, :, :, cols(h, q)], G.at[a, h, mine], s_g_s.at[a, h], s_g_r.at[a, h, k], dev(h, d, q))
+            send(OWN.at[a, :, :, cols(h, other)], G.at[a, h, mine], s_g_s.at[a, h], s_g_r.at[a, h, 4], dev(h, 0, other))
+            copy(OWN.at[a, :, :, cols(h, core)], G.at[a, h, mine], s_g_r.at[a, h, 5])
+
+    def gather_forward(a):
+        for h in (0, 1):
+            left = 2 * at(h, 3)
+            wait(G.at[a, h, pl.ds(left, 2)], s_g_r.at[a, h, 0])
+            for k in (0, 1):
+                part = G.at[a, h, left + k, pl.ds(0, 4)]
+                send(part, part, s_g_s.at[a, h], s_g_r.at[a, h, 2], dev(h, 1, core))
+        for h in (0, 1):
+            right = 2 * at(h, 1)
+            wait(G.at[a, h, pl.ds(right, 2)], s_g_r.at[a, h, 1])
+            for k in (0, 1):
+                part = G.at[a, h, right + k, pl.ds(4, 4)]
+                send(part, part, s_g_s.at[a, h], s_g_r.at[a, h, 3], dev(h, 3, core))
+
+    def gather_finish(a, h):
+        far = 2 * at(h, 2)
+        wait(G.at[a, h, pl.ds(far, 2), pl.ds(0, 4)], s_g_r.at[a, h, 2])
+        wait(G.at[a, h, pl.ds(far, 2), pl.ds(4, 4)], s_g_r.at[a, h, 3])
+        wait(G.at[a, h, ring[h] * 2 + other], s_g_r.at[a, h, 4])
+        wait(G.at[a, h, ring[h] * 2 + core], s_g_r.at[a, h, 5])
+
+    def gather_sent(a):
+        for h in (0, 1):
+            wait(G.at[a, h, pl.ds(0, 7)], s_g_s.at[a, h])
+
+    wait(OWN.at[0], s_o.at[0])
+    gather_start(0)
+    copy(wd, WD, s_w.at[2])
+    copy(wg, WG, s_w.at[0])
+    copy(wu, WU, s_w.at[1])
+    wait(OWN.at[2], s_o.at[2])
+    normalize(2)
+
     def experts(h):
         e = up // 16
         if h == 0:
@@ -199,9 +203,11 @@
 
     for h in (0, 1):
         wait(RG.at[h], s_rg_r.at[h])
-    for st in (1, 0):
-        for h in (0, 1):
-            build(st, h)
+    for h in (0, 1):
+        build(1, h)
+    gather_start(1)
+    for h in (0, 1):
+        build(0, h)
 
     def pack(a, st, h, b, gated):
         def body(i, carry):
@@ -243,17 +249,30 @@
 
     gather_forward(0)
     for h in (0, 1):
+
+        def turn(s, carry):
+            for k, T in enumerate((PB, PA)):
+                spot = pl.ds(128 * k, 128)
+                PT[h, s, :, spot] = dot_nt(EYE[...], T[1, h, s]).astype(BF)
+                for n, part in enumerate(split(T[0, h, s].astype(F32) * gates(0, h, s))):
+                    PG[n, h, s, :, spot] = dot_nt(EYE[...], part).astype(BF)
+            return carry
+
+        lax.fori_loop(0, 8, turn, 0)
+
+    gather_forward(1)
+    gather_start(2)
+    for h in (0, 1):
         gather_finish(0, h)
         pack(0, 1, h, 0, True)
         scatter_start(0, h, 0)
-    gather_start(2)
-    gather_forward(1)
     gather_sent(0)
     for h in (0, 1):
         gather_finish(1, h)
         pack(1, 1, h, 1, False)
+    gather_forward(2)
+    for h in (0, 1):
         scatter_start(1, h, 1)
-    gather_forward(2)
     gather_sent(1)
     scatter_sent(0, 0)
     for h in (0, 1):
@@ -281,9 +300,16 @@
 
     scatter_finish(0, 0)
     exchange(0)
+    wait(WD, s_w.at[2])
+
+    def early_hidden(f, carry):
+        at_cols = pl.ds(pl.multiple_of(f * STEP, STEP), STEP)
+        HID[:, at_cols] = dot_nt(rows(XA[0]), WD[at_cols, pl.ds(0, HALF)]) + dot_nt(rows(YB[0]), WD[at_cols, pl.ds(HALF, HALF)])
+        return carry
+
+    lax.fori_loop(0, FE // STEP, early_hidden, 0)
     wait(WG, s_w.at[0])
     wait(WU, s_w.at[1])
-    wait(WD, s_w.at[2])
     scatter_finish(1, 1)
     scatter_sent(1, 1)
     exchange(1)
@@ -295,7 +321,7 @@
         at_cols = pl.ds(pl.multiple_of(f * STEP, STEP), STEP)
         pre_gate = into(1, WG, at_cols)
         pre_up = into(1, WU, at_cols)
-        hidden = dot_nt(rows(XA[0]), WD[at_cols, pl.ds(0, HALF)]) + dot_nt(rows(YB[0]), WD[at_cols, pl.ds(HALF, HALF)])
+        hidden = HID[:, at_cols]
         sig = 1.0 / (1.0 + jnp.exp(-pre_gate))
         GG[:, at_cols] = (hidden * pre_up * sig * (1.0 + pre_gate * (1.0 - sig))).astype(BF)
         UG[:, at_cols] = (hidden * pre_gate * sig).astype(BF)
@@ -349,7 +375,8 @@
 
     lax.fori_loop(0, FE // STEP, forward_hidden, 0)
     exchange_hidden(GG, XA)
-    for ch, (c0, cw) in enumerate(CHUNKS):
+    def forward_out(ch):
+        c0, cw = CHUNKS[ch]
         for h in (0, 1):
             for q in (0, 1):
                 for n in range(0, cw, STEP):
@@ -357,32 +384,34 @@
                     act = GG[...] if h == 0 else rows(XA[1, :, :, pl.ds(0, FE)])
                     start = q * QUARTER + c0 + n
                     X[h][2, :, :, pl.ds(start, w)] = tiles(dot(act, WD[:, pl.ds(h * HALF + start, w)]).astype(BF))
+
+    def forward_return(ch):
+        for h in (0, 1):
             return_start(1, ch, h, 2)
+
+    forward_out(0)
+    forward_return(0)
+    forward_out(1)
+    forward_out(2)
 
     copy(bin_, OWN.at[1], s_o.at[1])
     copy(fin, OWN.at[2], s_o.at[2])
 
-    def combine(b, ch, h):
+    def combine(b, ch, h, ds):
         c0, cw = (0, QUARTER) if b == 0 else CHUNKS[ch]
-        st, to = (1, 1) if b == 0 else (0, 0)
+        to = 1 if b == 0 else 0
         here = pl.ds(c0, cw)
-
-        def body(s, carry):
-            prev = rows(G[b, h, jnp.maximum(s - 1, 0), :, :, here])
-            cur = rows(G[b, h, jnp.minimum(s, 6), :, :, here])
-            pa, pb = PA[st, h, s], PB[st, h, s]
-            if b == 0:
-                out = dot(dot_nt(EYE[...], pb).astype(BF), prev) + dot(dot_nt(EYE[...], pa).astype(BF), cur)
-            else:
-                weight = gates(st, h, s)
-                out = 0.0
-                for pick, block in ((pb, prev), (pa, cur)):
-                    for part in split(pick.astype(F32) * weight):
-                        out = out + dot(dot_nt(EYE[...], part).astype(BF), block)
-            S[to, h, s, :, :, here] = tiles(out.astype(BF))
-            return carry
-
-        lax.fori_loop(0, 8, body, 0)
+        for d in ds:
+            for k in (0, 1):
+                s = 2 * at(h, d) + k
+                prev = rows(G[b, h, jnp.maximum(s - 1, 0), :, :, here])
+                cur = rows(G[b, h, jnp.minimum(s, 6), :, :, here])
+                both = jnp.concatenate([prev, cur], axis=0)
+                if b == 0:
+                    out = dot(PT[h, s], both)
+                else:
+                    out = dot(PG[0, h, s], both) + dot(PG[1, h, s], both)
+                S[to, h, s, :, :, here] = tiles(out.astype(BF))
 
     def land(b):
         return L if b == 0 else G.at[2]
@@ -394,9 +423,14 @@
     def far_start(b, ch, h):
         n, here, to, B = meta(b, ch)
         far = 2 * at(h, 2)
+        combine(b, ch, h, (2,))
         for k in (0, 1):
             send(S.at[to, h, far + k, pl.ds(0, 4), :, here], B.at[h, 6, pl.ds(4 * k, 4), :, here], s_t1_s.at[n, h], s_t1_r.at[n, h, 0], dev(h, 1, core))
             send(S.at[to, h, far + k, pl.ds(4, 4), :, here], B.at[h, 7, pl.ds(4 * k, 4), :, here], s_t1_s.at[n, h], s_t1_r.at[n, h, 1], dev(h, 3, core))
+
+    def own_start(b, ch, h):
+        n, here, to, B = meta(b, ch)
+        combine(b, ch, h, (1, 3, 0))
         send(S.at[to, h, 2 * ring[h] + other, :, :, here], B.at[h, 4 + core, :, :, here], s_t2_s.at[n, h], s_c_r.at[n, h, 0], dev(h, 0, other))
         copy(S.at[to, h, 2 * ring[h] + core, :, :, here], B.at[h, 4 + core, :, :, here], s_c_r.at[n, h, 1])
 
@@ -423,21 +457,27 @@
 
     for h in (0, 1):
         wait(G.at[0, h, pl.ds(0, 7)], s_r_r.at[0, h])
-        combine(0, 0, h)
         far_start(0, 0, h)
     for h in (0, 1):
+        own_start(0, 0, h)
+    def relay_far(ch):
+        n, here, to, B = meta(1, ch)
+        for h in (0, 1):
+            wait(G.at[1, h, pl.ds(0, 7), :, :, here], s_r_r.at[n, h])
+            far_start(1, ch, h)
+        for h in (0, 1):
+            own_start(1, ch, h)
+
+    def relay_near(ch):
+        for h in (0, 1):
+            near_start(1, ch, h)
+
+    relay_far(0)
+    for h in (0, 1):
         near_start(0, 0, h)
-
-    def forward_relay(ch):
-        n, here, to, B = meta(1, ch)
-        for h in (0, 1):
-            wait(G.at[1, h, pl.ds(0, 7), :, :, here], s_r_r.at[n, h])
-            combine(1, ch, h)
-            far_start(1, ch, h)
-        for h in (0, 1):
-            near_start(1, ch, h)
-
-    forward_relay(0)
+    relay_near(0)
+    forward_return(1)
+    forward_return(2)
 
     for h in (0, 1):
         near_finish(0, 0, h)
@@ -448,7 +488,7 @@
         summed = jnp.concatenate([arrived(0, h, q, k, pl.ds(0, QUARTER)) for h in (0, 1) for q in (0, 1)], axis=1)
         stored = OWN[1, k].astype(F32)
         r = lax.rsqrt(jnp.mean(stored * stored, axis=-1, keepdims=True) + EPSILON)
-        grad = gain[...] * summed
+        grad = gain[...].astype(F32) * summed
         mean = jnp.mean(stored * grad, axis=-1, keepdims=True)
         OWN[1, k] = (OWN[0, k].astype(F32) + r * grad - stored * (r * r * r) * mean).astype(BF)
         return carry
@@ -473,10 +513,13 @@
                 spot = pl.ds(h * HALF + q * QUARTER + c0, cw)
                 send(OWN.at[2, :, :, spot], fo.at[:, :, spot], s_y_s.at[1 + ch], s_y_r.at[1 + ch], ahead)
 
-    for ch in range(1, len(CHUNKS)):
-        forward_relay(ch)
-        forward_last(ch - 1)
-    forward_last(len(CHUNKS) - 1)
+    forward_last(0)
+    relay_far(1)
+    relay_far(2)
+    relay_near(1)
+    forward_last(1)
+    relay_near(2)
+    forward_last(2)
 
     for h in (0, 1):
         wait(RG.at[h, pl.ds(0, 7)], s_rg_s.at[h])
@@ -494,6 +537,18 @@
         wait(fo.at[:, :, pl.ds(0, 4 * cw)], s_y_r.at[1 + ch])
 
 
+def hand_over(fo, bo, f_out, b_out, held, sem):
+    loads = [pltpu.make_async_copy(a, held.at[i], sem.at[i]) for i, a in enumerate((fo, bo))]
+    stores = [pltpu.make_async_copy(held.at[i], a, sem.at[2 + i]) for i, a in enumerate((f_out, b_out))]
+    for copy in loads:
+        copy.start()
+    for load, store in zip(loads, stores):
+        load.wait()
+        store.start()
+    for copy in stores:
+        copy.wait()
+
+
 def local(
     forward_input,
     forward_routes,
@@ -507,9 +562,6 @@
     up_weight,
     down_weight,
 ):
-    rg = jnp.concatenate(
-        [forward_routes[0].astype(F32), forward_gates[0], backward_routes[0].astype(F32), backward_gates[0]], axis=1
-    ).T
     shape = (8, 16, D)
     parts = 1 + len(CHUNKS)
     groups = 2 * len(CHUNKS)
@@ -520,7 +572,7 @@
         kernel,
         name="relay",
         out_shape=(jax.ShapeDtypeStruct(shape, BF), jax.ShapeDtypeStruct(shape, BF)),
-        in_specs=[vmem, anywhere, anywhere, anywhere, vmem, anywhere, anywhere, anywhere],
+        in_specs=[vmem] * 4 + [anywhere] * 3 + [vmem] + [anywhere] * 3,
         out_specs=(anywhere, anywhere),
         scratch_shapes=[
             pltpu.VMEM((D, FE), BF),
@@ -537,9 +589,13 @@
             pltpu.VMEM((2, 2, 8, 128, 128), BF),
             pltpu.VMEM((448, FE), BF),
             pltpu.VMEM((448, FE), BF),
+            pltpu.VMEM((448, FE), F32),
             pltpu.VMEM((448, 448), BF),
             pltpu.VMEM((128, 128), BF),
             pltpu.VMEM((128, 128), BF),
+            pltpu.VMEM((2, 8, 128, 256), BF),
+            pltpu.VMEM((2, 2, 8, 128, 256), BF),
+            pltpu.VMEM((8, 128), F32),
             dma((2,)),
             dma((2,)),
             dma((3, 2, 6)),
@@ -564,15 +620,27 @@
         ),
         cost_estimate=pl.CostEstimate(flops=46 * 10**9, bytes_accessed=30 * 10**6, transcendentals=10**6),
     )(
-        rg,
+        forward_routes[0].T,
+        forward_gates[0].T,
+        backward_routes[0].T,
+        backward_gates[0].T,
         forward_input.reshape(shape),
         backward_input.reshape(shape),
         upstream_gradient.reshape(shape),
-        norm_gain.astype(F32),
+        norm_gain,
         gate_weight[0, 0],
         up_weight[0, 0],
         down_weight[0, 0],
     )
+    fo, bo = pl.pallas_call(
+        hand_over,
+        name="results",
+        out_shape=(jax.ShapeDtypeStruct(shape, BF), jax.ShapeDtypeStruct(shape, BF)),
+        in_specs=[anywhere] * 2,
+        out_specs=(anywhere, anywhere),
+        scratch_shapes=[pltpu.VMEM((2,) + shape, BF), dma((4,))],
+        cost_estimate=pl.CostEstimate(flops=0, bytes_accessed=4 * 10**6, transcendentals=0),
+    )(fo, bo)
     return (fo.reshape(1, 128, D), bo.reshape(1, 128, D))
 
 

time: 236 us -> 194 us (0.82)
  Pallas kernels: 227 us -> 192 us
  local copies, waits for them, and re-layouts: 4.32 us -> 0 us
  other arithmetic: 3.32 us -> 0 us
    pallas_call x1, Pallas kernels: 227 us -> 189 us  [local(): pl.pallas_call(kernel, name='relay', out_shape=(jax.ShapeDtypeStruct(shap...]
    unnamed x2 -> x0, local copies, waits for them, and re-layouts: 4.32 us -> none
    pallas_call x0 -> x1, Pallas kernels: none -> 2.44 us  [local(): pl.pallas_call(hand_over, name='results', out_shape=(jax.ShapeDtypeStruct...]
where the time goes in v2:
time: 194 us; the launch traced here: 193 us
  Pallas kernels  192 us (99%)
    pallas_call x1, Pallas kernels, local(): pl.pallas_call(kernel, name='relay', out_shape=(jax.ShapeDtypeStruct(shap...  189 us

profile of v2, /device:TPU:0, one launch (start us, length us, event | category | flops | bytes accessed | tf_op | source)
XLA Modules:
  0.0 192.7 jit_solution(16802207989779859373)
XLA Ops:
  0.6 189.5 %relay.1 = (bf16[8,16,3584]{2,1,0:T(8,128)(2,1)}, bf16[8,16,3584]{2,1,0:T(8,128)(2,1)}) custom-call(s32[2,128]{1,0:T(2,128)} %bitcast.28, f32[2,128]{1,0:T(2,128)} %bitcast.29, s32[2,128]{1,0:T(2,128)} %bitcast.30, f32[2,128]{1,0:T(2,128)} %bitcast.31, bf16[8,16,3584]{2,1,0:T(8,128)(2,1)} %bitcast.23, bf16[8,16,3584]{2,1,0:T(8,128)(2,1)} %bitcast.24, ...), custom_call_target="tpu_custom_call" | custom-call | flops 46000001024 | bytes 30000000 | tf_op jit(solution)/shard_map/relay/pallas_call | solution.py:571
  190.1 2.4 %results.1 = (bf16[8,16,3584]{2,1,0:T(8,128)(2,1)}, bf16[8,16,3584]{2,1,0:T(8,128)(2,1)}) custom-call(bf16[8,16,3584]{2,1,0:T(8,128)(2,1)} %get-tuple-element.6.fo, bf16[8,16,3584]{2,1,0:T(8,128)(2,1)} %get-tuple-element.7.bo), custom_call_target="tpu_custom_call" | custom-call | bytes 4000000 | tf_op jit(solution)/shard_map/results/pallas_call | solution.py:635

commit v3 on v2

--- a/solution.py
+++ b/solution.py
@@ -17,8 +17,10 @@
 QUARTER = D // 4
 SIDE = 4
 SLOTS = 14
-CHUNKS = ((0, 512), (512, 256), (768, 128))
+CHUNKS = ((0, 384), (384, 256), (640, 128), (768, 128))
+DIRECT = (2, 3)
 STEP = 256
+WIDE = 512
 
 
 def dot(a, b):
@@ -107,8 +109,6 @@
 
         lax.fori_loop(0, 8, body, 0)
 
-    wait(OWN.at[1], s_o.at[1])
-    normalize(1)
     up = lax.broadcasted_iota(jnp.int32, (128, 128), 0)
     across = lax.broadcasted_iota(jnp.int32, (128, 128), 1)
     TRI[...] = jnp.where(up < across, 1.0, 0.0).astype(BF)
@@ -166,6 +166,8 @@
 
     wait(OWN.at[0], s_o.at[0])
     gather_start(0)
+    wait(OWN.at[1], s_o.at[1])
+    normalize(1)
     copy(wd, WD, s_w.at[2])
     copy(wg, WG, s_w.at[0])
     copy(wu, WU, s_w.at[1])
@@ -284,19 +286,19 @@
 
     def exchange(a):
         def body(n, carry):
-            at_cols = pl.ds(pl.multiple_of(n * STEP, STEP), STEP)
+            at_cols = pl.ds(pl.multiple_of(n * 896, 896), 896)
             YB[a, :, :, at_cols] = tiles(dot(PERM[...], rows(YB[a, :, :, at_cols])).astype(BF))
             return carry
 
-        lax.fori_loop(0, HALF // STEP, body, 0)
+        lax.fori_loop(0, HALF // 896, body, 0)
 
     def exchange_hidden(src, dst):
         def body(n, carry):
-            at_cols = pl.ds(pl.multiple_of(n * STEP, STEP), STEP)
+            at_cols = pl.ds(pl.multiple_of(n * WIDE, WIDE), WIDE)
             dst[1, :, :, at_cols] = tiles(dot(PERM[...], src[:, at_cols]).astype(BF))
             return carry
 
-        lax.fori_loop(0, FE // STEP, body, 0)
+        lax.fori_loop(0, FE // WIDE, body, 0)
 
     scatter_finish(0, 0)
     exchange(0)
@@ -331,25 +333,24 @@
     exchange_hidden(GG, XA)
     exchange_hidden(UG, YB)
 
-    def return_start(b, ch, h, a):
-        c0, cw = ((0, QUARTER),) [0] if b == 0 else CHUNKS[ch]
-        gb = b
+    def return_start(b, ch, h, a, quarters=(0, 1), home=True):
+        c0, cw = (0, QUARTER) if b == 0 else CHUNKS[ch]
         mine = 2 * ring[1 - h] + core
         n = b * len(CHUNKS) + ch
-        dst = G.at[gb, h, pl.ds(0, 7), mine, :, pl.ds(c0, cw)]
+        dst = G.at[b, h, pl.ds(0, 7), mine, :, pl.ds(c0, cw)]
         for d in (1, 3, 2):
-            for q in (0, 1):
+            for q in quarters:
                 send(
                     X[h].at[a, pl.ds(7 * at(1 - h, d), 7), :, qcols(q, c0, cw)], dst,
                     s_r_s.at[n, h], s_r_r.at[n, h], dev(1 - h, d, q),
                 )
-        home = pl.ds(7 * ring[1 - h], 7)
-        send(X[h].at[a, home, :, qcols(other, c0, cw)], dst, s_r_s.at[n, h], s_r_r.at[n, h], dev(1 - h, 0, other))
-        copy(X[h].at[a, home, :, qcols(core, c0, cw)], dst, s_r_r.at[n, h])
-
-    for h in (0, 1):
-
-        def backward_out(n, carry):
+        if home:
+            here = pl.ds(7 * ring[1 - h], 7)
+            send(X[h].at[a, here, :, qcols(other, c0, cw)], dst, s_r_s.at[n, h], s_r_r.at[n, h], dev(1 - h, 0, other))
+            copy(X[h].at[a, here, :, qcols(core, c0, cw)], dst, s_r_r.at[n, h])
+
+    def backward_out(h, first, last):
+        def body(n, carry):
             at_rows = pl.ds(pl.multiple_of(h * HALF + n * STEP, STEP), STEP)
             at_cols = pl.ds(pl.multiple_of(n * STEP, STEP), STEP)
             if h == 0:
@@ -359,8 +360,13 @@
             X[h][0, :, :, at_cols] = tiles((dot_nt(gg, WG[at_rows, :]) + dot_nt(ug, WU[at_rows, :])).astype(BF))
             return carry
 
-        lax.fori_loop(0, HALF // STEP, backward_out, 0)
-        return_start(0, 0, h, 0)
+        lax.fori_loop(first, last, body, 0)
+
+    for q, first, last in ((0, 0, 4), (1, 4, HALF // STEP)):
+        for h in (0, 1):
+            backward_out(h, first, last)
+        for h in (0, 1):
+            return_start(0, 0, h, 0, (q,), q == 1)
 
     scatter_finish(2, 0)
     scatter_sent(2, 0)
@@ -391,8 +397,6 @@
 
     forward_out(0)
     forward_return(0)
-    forward_out(1)
-    forward_out(2)
 
     copy(bin_, OWN.at[1], s_o.at[1])
     copy(fin, OWN.at[2], s_o.at[2])
@@ -428,9 +432,9 @@
             send(S.at[to, h, far + k, pl.ds(0, 4), :, here], B.at[h, 6, pl.ds(4 * k, 4), :, here], s_t1_s.at[n, h], s_t1_r.at[n, h, 0], dev(h, 1, core))
             send(S.at[to, h, far + k, pl.ds(4, 4), :, here], B.at[h, 7, pl.ds(4 * k, 4), :, here], s_t1_s.at[n, h], s_t1_r.at[n, h, 1], dev(h, 3, core))
 
-    def own_start(b, ch, h):
+    def own_start(b, ch, h, ds=(1, 3, 0)):
         n, here, to, B = meta(b, ch)
-        combine(b, ch, h, (1, 3, 0))
+        combine(b, ch, h, ds)
         send(S.at[to, h, 2 * ring[h] + other, :, :, here], B.at[h, 4 + core, :, :, here], s_t2_s.at[n, h], s_c_r.at[n, h, 0], dev(h, 0, other))
         copy(S.at[to, h, 2 * ring[h] + core, :, :, here], B.at[h, 4 + core, :, :, here], s_c_r.at[n, h, 1])
 
@@ -445,15 +449,31 @@
                 S[to, h, near + k, pl.ds(t0, 4), :, here] = (own + got).astype(BF)
                 send(S.at[to, h, near + k, :, :, here], B.at[h, base + core, :, :, here], s_t2_s.at[n, h], s_t2_r.at[n, h], dev(h, d, k))
 
+    def relay_direct(ch):
+        n, here, to, B = meta(1, ch)
+        for h in (0, 1):
+            wait(G.at[1, h, pl.ds(0, 7), :, :, here], s_r_r.at[n, h])
+        for d, base in ((2, 6), (1, 0), (3, 2)):
+            for h in (0, 1):
+                combine(1, ch, h, (d,))
+                for k in (0, 1):
+                    ss, rs = (s_t1_s.at[n, h], s_t1_r.at[n, h, 0]) if d == 2 else (s_t2_s.at[n, h], s_t2_r.at[n, h])
+                    send(S.at[to, h, 2 * at(h, d) + k, :, :, here], B.at[h, base + core, :, :, here], ss, rs, dev(h, d, k))
+        for h in (0, 1):
+            own_start(1, ch, h, (0,))
+
     def near_finish(b, ch, h):
         n, here, to, B = meta(b, ch)
+        if b == 1 and ch in DIRECT:
+            wait(B.at[h, pl.ds(6, 2), :, :, here], s_t1_r.at[n, h, 0])
         wait(B.at[h, pl.ds(0, 4), :, :, here], s_t2_r.at[n, h])
         wait(B.at[h, 4 + other, :, :, here], s_c_r.at[n, h, 0])
         wait(B.at[h, 4 + core, :, :, here], s_c_r.at[n, h, 1])
 
-    def arrived(b, h, q, k, here):
+    def arrived(b, h, q, k, here, direct=False):
         B = land(b)
-        return B[h, q, k, :, here].astype(F32) + B[h, 2 + q, k, :, here].astype(F32) + B[h, 4 + q, k, :, here].astype(F32)
+        far = B[h, 6 + q, k, :, here].astype(F32) if direct else 0.0
+        return far + B[h, q, k, :, here].astype(F32) + B[h, 2 + q, k, :, here].astype(F32) + B[h, 4 + q, k, :, here].astype(F32)
 
     for h in (0, 1):
         wait(G.at[0, h, pl.ds(0, 7)], s_r_r.at[0, h])
@@ -472,17 +492,40 @@
         for h in (0, 1):
             near_start(1, ch, h)
 
+    forward_out(1)
     relay_far(0)
+    forward_return(1)
+    forward_out(2)
+    forward_out(3)
+    relay_near(0)
     for h in (0, 1):
         near_start(0, 0, h)
-    relay_near(0)
-    forward_return(1)
+    relay_far(1)
     forward_return(2)
-
-    for h in (0, 1):
-        near_finish(0, 0, h)
+    forward_return(3)
+
+    def forward_last(ch):
+        c0, cw = CHUNKS[ch]
+        n, here, to, B = meta(1, ch)
+        for h in (0, 1):
+            near_finish(1, ch, h)
+
+            def body(k, carry):
+                for q in (0, 1):
+                    spot = pl.ds(h * HALF + q * QUARTER + c0, cw)
+                    OWN[2, k, :, spot] = (OWN[2, k, :, spot].astype(F32) + arrived(1, h, q, k, here, ch in DIRECT)).astype(BF)
+                return carry
+
+            lax.fori_loop(0, 8, body, 0)
+            for q in (0, 1):
+                spot = pl.ds(h * HALF + q * QUARTER + c0, cw)
+                send(OWN.at[2, :, :, spot], fo.at[:, :, spot], s_y_s.at[1 + ch], s_y_r.at[1 + ch], ahead)
+
     wait(OWN.at[1], s_o.at[1])
     wait(OWN.at[2], s_o.at[2])
+    forward_last(0)
+    for h in (0, 1):
+        near_finish(0, 0, h)
 
     def backward_last(k, carry):
         summed = jnp.concatenate([arrived(0, h, q, k, pl.ds(0, QUARTER)) for h in (0, 1) for q in (0, 1)], axis=1)
@@ -493,33 +536,17 @@
         OWN[1, k] = (OWN[0, k].astype(F32) + r * grad - stored * (r * r * r) * mean).astype(BF)
         return carry
 
-    lax.fori_loop(0, 8, backward_last, 0)
-    send(OWN.at[1], bo, s_y_s.at[0], s_y_r.at[0], behind)
-
-    def forward_last(ch):
-        c0, cw = CHUNKS[ch]
-        n, here, to, B = meta(1, ch)
-        for h in (0, 1):
-            near_finish(1, ch, h)
-
-            def body(k, carry):
-                for q in (0, 1):
-                    spot = pl.ds(h * HALF + q * QUARTER + c0, cw)
-                    OWN[2, k, :, spot] = (OWN[2, k, :, spot].astype(F32) + arrived(1, h, q, k, here)).astype(BF)
-                return carry
-
-            lax.fori_loop(0, 8, body, 0)
-            for q in (0, 1):
-                spot = pl.ds(h * HALF + q * QUARTER + c0, cw)
-                send(OWN.at[2, :, :, spot], fo.at[:, :, spot], s_y_s.at[1 + ch], s_y_r.at[1 + ch], ahead)
-
-    forward_last(0)
-    relay_far(1)
-    relay_far(2)
+    for first in (0, 4):
+        lax.fori_loop(first, first + 4, backward_last, 0)
+        part = pl.ds(first, 4)
+        send(OWN.at[1, part], bo.at[part], s_y_s.at[0], s_y_r.at[0], behind)
+
     relay_near(1)
+    relay_direct(2)
     forward_last(1)
-    relay_near(2)
+    relay_direct(3)
     forward_last(2)
+    forward_last(3)
 
     for h in (0, 1):
         wait(RG.at[h, pl.ds(0, 7)], s_rg_s.at[h])
@@ -538,8 +565,9 @@
 
 
 def hand_over(fo, bo, f_out, b_out, held, sem):
-    loads = [pltpu.make_async_copy(a, held.at[i], sem.at[i]) for i, a in enumerate((fo, bo))]
-    stores = [pltpu.make_async_copy(held.at[i], a, sem.at[2 + i]) for i, a in enumerate((f_out, b_out))]
+    parts = [(i, pl.ds(4 * k, 4)) for i in (0, 1) for k in (0, 1)]
+    loads = [pltpu.make_async_copy((fo, bo)[i].at[at], held.at[i, at], sem.at[0, n]) for n, (i, at) in enumerate(parts)]
+    stores = [pltpu.make_async_copy(held.at[i, at], (f_out, b_out)[i].at[at], sem.at[1, n]) for n, (i, at) in enumerate(parts)]
     for copy in loads:
         copy.start()
     for load, store in zip(loads, stores):
@@ -638,7 +666,7 @@
         out_shape=(jax.ShapeDtypeStruct(shape, BF), jax.ShapeDtypeStruct(shape, BF)),
         in_specs=[anywhere] * 2,
         out_specs=(anywhere, anywhere),
-        scratch_shapes=[pltpu.VMEM((2,) + shape, BF), dma((4,))],
+        scratch_shapes=[pltpu.VMEM((2,) + shape, BF), dma((2, 4))],
         cost_estimate=pl.CostEstimate(flops=0, bytes_accessed=4 * 10**6, transcendentals=0),
     )(fo, bo)
     return (fo.reshape(1, 128, D), bo.reshape(1, 128, D))

time: 194 us -> 187 us (0.964)
  Pallas kernels: 192 us -> 183 us
    pallas_call x1, Pallas kernels: 189 us -> 181 us  [local(): pl.pallas_call(kernel, name='relay', out_shape=(jax.ShapeDtypeStruct(shap...]
where the time goes in v3:
time: 187 us; the launch traced here: 184 us
  Pallas kernels  183 us (98%)
    pallas_call x1, Pallas kernels, local(): pl.pallas_call(kernel, name='relay', out_shape=(jax.ShapeDtypeStruct(shap...  181 us

profile of v3, /device:TPU:0, one launch (start us, length us, event | category | flops | bytes accessed | tf_op | source)
XLA Modules:
  0.0 183.9 jit_solution(2399683432020559202)
XLA Ops:
  0.6 180.8 %relay.1 = (bf16[8,16,3584]{2,1,0:T(8,128)(2,1)}, bf16[8,16,3584]{2,1,0:T(8,128)(2,1)}) custom-call(s32[2,128]{1,0:T(2,128)} %bitcast.28, f32[2,128]{1,0:T(2,128)} %bitcast.29, s32[2,128]{1,0:T(2,128)} %bitcast.30, f32[2,128]{1,0:T(2,128)} %bitcast.31, bf16[8,16,3584]{2,1,0:T(8,128)(2,1)} %bitcast.23, bf16[8,16,3584]{2,1,0:T(8,128)(2,1)} %bitcast.24, ...), custom_call_target="tpu_custom_call" | custom-call | flops 46000001024 | bytes 30000000 | tf_op jit(solution)/shard_map/relay/pallas_call | solution.py:599
  181.5 2.3 %results.1 = (bf16[8,16,3584]{2,1,0:T(8,128)(2,1)}, bf16[8,16,3584]{2,1,0:T(8,128)(2,1)}) custom-call(bf16[8,16,3584]{2,1,0:T(8,128)(2,1)} %get-tuple-element.6.fo, bf16[8,16,3584]{2,1,0:T(8,128)(2,1)} %get-tuple-element.7.bo), custom_call_target="tpu_custom_call" | custom-call | bytes 4000000 | tf_op jit(solution)/shard_map/results/pallas_call | solution.py:663

commit v4 on v3

--- a/solution.py
+++ b/solution.py
@@ -19,6 +19,7 @@
 SLOTS = 14
 CHUNKS = ((0, 384), (384, 256), (640, 128), (768, 128))
 DIRECT = (2, 3)
+PARTS = ((0, 3), (3, 1))
 STEP = 256
 WIDE = 512
 
@@ -45,10 +46,10 @@
 
 
 def kernel(
-    fr, fg, br, bg, fin, bin_, upg, gain, wg, wu, wd, fo, bo,
-    WG, WU, WD, G, XA, YB, S, L, OWN, RG, PA, PB, GG, UG, HID, PERM, TRI, EYE, PT, PG, rg,
+    fr_in, fg_in, br_in, bg_in, fin, bin_, upg, gain_in, wg, wu, wd, fo, bo,
+    WG, WU, WD, G, XA, YB, S, L, OWN, RG, PA, PB, GG, UG, HID, PERM, PT, PG, rg, fr, fg, br, bg, gain,
     s_rg_r, s_rg_s, s_g_r, s_g_s, s_x_r, s_x_s, s_r_r, s_r_s,
-    s_t1_r, s_t1_s, s_t2_r, s_t2_s, s_c_r, s_y_r, s_y_s, s_w, s_o, s_l,
+    s_t1_r, s_t1_s, s_t2_r, s_t2_s, s_c_r, s_y_r, s_y_s, s_w, s_o, s_l, s_i,
 ):
     pipe = lax.axis_index("pipe")
     me = lax.axis_index("expert")
@@ -82,15 +83,6 @@
 
     def wait(ref, sem):
         pltpu.make_async_copy(ref, ref, sem).wait()
-
-    copy(upg, OWN.at[0], s_o.at[0])
-    copy(bin_, OWN.at[1], s_o.at[1])
-    copy(fin, OWN.at[2], s_o.at[2])
-
-    rg[pl.ds(0, 2), :] = fr[...].astype(F32)
-    rg[pl.ds(2, 2), :] = fg[...]
-    rg[pl.ds(4, 2), :] = br[...].astype(F32)
-    rg[pl.ds(6, 2), :] = bg[...]
 
     barrier = pltpu.get_barrier_semaphore()
     peers = [dev(h, d, k) for h in (0, 1) for d in (1, 2, 3) for k in (0, 1)]
@@ -109,10 +101,24 @@
 
         lax.fori_loop(0, 8, body, 0)
 
+    copy(upg, OWN.at[0], s_o.at[0])
+    copy(bin_, OWN.at[1], s_o.at[1])
+    copy(fin, OWN.at[2], s_o.at[2])
+
+    small = ((fr_in, fr), (fg_in, fg), (br_in, br), (bg_in, bg), (gain_in, gain))
+    for n, (src, dst) in enumerate(small):
+        copy(src, dst, s_i.at[n])
+    for n, (src, dst) in enumerate(small):
+        wait(dst, s_i.at[n])
+    rg[pl.ds(0, 2), :] = fr[...].astype(F32)
+    rg[pl.ds(2, 2), :] = fg[...]
+    rg[pl.ds(4, 2), :] = br[...].astype(F32)
+    rg[pl.ds(6, 2), :] = bg[...]
+
     up = lax.broadcasted_iota(jnp.int32, (128, 128), 0)
     across = lax.broadcasted_iota(jnp.int32, (128, 128), 1)
-    TRI[...] = jnp.where(up < across, 1.0, 0.0).astype(BF)
-    EYE[...] = jnp.where(up == across, 1.0, 0.0).astype(BF)
+    triangle = jnp.where(up < across, 1.0, 0.0).astype(BF)
+    identity = jnp.where(up == across, 1.0, 0.0).astype(BF)
     line = lax.broadcasted_iota(jnp.int32, (448, 448), 0)
     outer = (line >= 112).astype(jnp.int32) + (line >= 224).astype(jnp.int32) + (line >= 336).astype(jnp.int32)
     rest = line - 112 * outer
@@ -192,7 +198,7 @@
         def body(s, carry):
             named = (route_row(h, s, 4 * st) == ids[h]) | (route_row(h, s, 4 * st + 1) == ids[h])
             mask = jnp.where(named, 1.0, 0.0)
-            before = dot(mask.astype(BF), TRI[...])
+            before = dot(mask.astype(BF), triangle)
             first = 2.0 * s.astype(F32) + in_tile
             PA[st, h, s] = jnp.where(before == first, mask, 0.0).astype(BF)
             PB[st, h, s] = jnp.where(before == first - 16.0, mask, 0.0).astype(BF)
@@ -255,9 +261,9 @@
         def turn(s, carry):
             for k, T in enumerate((PB, PA)):
                 spot = pl.ds(128 * k, 128)
-                PT[h, s, :, spot] = dot_nt(EYE[...], T[1, h, s]).astype(BF)
+                PT[h, s, :, spot] = dot_nt(identity, T[1, h, s]).astype(BF)
                 for n, part in enumerate(split(T[0, h, s].astype(F32) * gates(0, h, s))):
-                    PG[n, h, s, :, spot] = dot_nt(EYE[...], part).astype(BF)
+                    PG[n, h, s, :, spot] = dot_nt(identity, part).astype(BF)
             return carry
 
         lax.fori_loop(0, 8, turn, 0)
@@ -449,6 +455,31 @@
                 S[to, h, near + k, pl.ds(t0, 4), :, here] = (own + got).astype(BF)
                 send(S.at[to, h, near + k, :, :, here], B.at[h, base + core, :, :, here], s_t2_s.at[n, h], s_t2_r.at[n, h], dev(h, d, k))
 
+    def stored_near(part):
+        n, here, to, B = meta(0, 0)
+        start, size = PARTS[part]
+        for h in (0, 1):
+            for slot, d, t0, base in ((6, 1, 0, 0), (7, 3, 4, 2)):
+                if part == 0:
+                    wait(B.at[h, slot], s_t1_r.at[n, h, slot - 6])
+                near = 2 * at(h, d)
+                for k in (0, 1):
+                    first = pl.ds(t0 + start, size)
+                    own = S[to, h, near + k, first].astype(F32)
+                    got = B[h, slot, pl.ds(4 * k + start, size)].astype(F32)
+                    S[to, h, near + k, first] = (own + got).astype(BF)
+                    for t in (0, 4):
+                        both = pl.ds(t + start, size)
+                        send(S.at[to, h, near + k, both], B.at[h, base + core, both], s_t2_s.at[part, h], s_t2_r.at[part, h], dev(h, d, k))
+
+    def stored_finish(part):
+        n, here, to, B = meta(0, 0)
+        for h in (0, 1):
+            wait(B.at[h, pl.ds(0, PARTS[part][1])], s_t2_r.at[part, h])
+            if part == 0:
+                wait(B.at[h, 4 + other], s_c_r.at[n, h, 0])
+                wait(B.at[h, 4 + core], s_c_r.at[n, h, 1])
+
     def relay_direct(ch):
         n, here, to, B = meta(1, ch)
         for h in (0, 1):
@@ -497,12 +528,10 @@
     forward_return(1)
     forward_out(2)
     forward_out(3)
+    stored_near(0)
     relay_near(0)
-    for h in (0, 1):
-        near_start(0, 0, h)
     relay_far(1)
     forward_return(2)
-    forward_return(3)
 
     def forward_last(ch):
         c0, cw = CHUNKS[ch]
@@ -520,12 +549,6 @@
             for q in (0, 1):
                 spot = pl.ds(h * HALF + q * QUARTER + c0, cw)
                 send(OWN.at[2, :, :, spot], fo.at[:, :, spot], s_y_s.at[1 + ch], s_y_r.at[1 + ch], ahead)
-
-    wait(OWN.at[1], s_o.at[1])
-    wait(OWN.at[2], s_o.at[2])
-    forward_last(0)
-    for h in (0, 1):
-        near_finish(0, 0, h)
 
     def backward_last(k, carry):
         summed = jnp.concatenate([arrived(0, h, q, k, pl.ds(0, QUARTER)) for h in (0, 1) for q in (0, 1)], axis=1)
@@ -536,15 +559,25 @@
         OWN[1, k] = (OWN[0, k].astype(F32) + r * grad - stored * (r * r * r) * mean).astype(BF)
         return carry
 
-    for first in (0, 4):
-        lax.fori_loop(first, first + 4, backward_last, 0)
-        part = pl.ds(first, 4)
-        send(OWN.at[1, part], bo.at[part], s_y_s.at[0], s_y_r.at[0], behind)
-
+    def stored_last(part):
+        stored_finish(part)
+        start, size = PARTS[part]
+        for first in (start, 4 + start):
+            lax.fori_loop(first, first + size, backward_last, 0)
+            both = pl.ds(first, size)
+            send(OWN.at[1, both], bo.at[both], s_y_s.at[0], s_y_r.at[0], behind)
+
+    wait(OWN.at[1], s_o.at[1])
+    wait(OWN.at[2], s_o.at[2])
+    stored_last(0)
+    forward_last(0)
     relay_near(1)
+    forward_return(3)
+    stored_near(1)
     relay_direct(2)
     forward_last(1)
     relay_direct(3)
+    stored_last(1)
     forward_last(2)
     forward_last(3)
 
@@ -556,7 +589,9 @@
             for h in (0, 1):
                 wait(S.at[to, h, pl.ds(0, 7), pl.ds(0, 7), :, here], s_r_s.at[n, h])
                 wait(S.at[to, h, pl.ds(0, 2), :, :, here], s_t1_s.at[n, h])
-                wait(S.at[to, h, pl.ds(0, 5), :, :, here], s_t2_s.at[n, h])
+                wait(S.at[to, h, pl.ds(0, 5 if b == 1 else 1 + PARTS[0][1]), :, :, here], s_t2_s.at[n, h])
+                if b == 0:
+                    wait(S.at[to, h, pl.ds(0, PARTS[1][1])], s_t2_s.at[1, h])
     wait(bo, s_y_s.at[0])
     wait(bo, s_y_r.at[0])
     for ch, (c0, cw) in enumerate(CHUNKS):
@@ -594,13 +629,12 @@
     parts = 1 + len(CHUNKS)
     groups = 2 * len(CHUNKS)
     dma = pltpu.SemaphoreType.DMA
-    vmem = pl.BlockSpec(memory_space=pltpu.VMEM)
     anywhere = pl.BlockSpec(memory_space=pl.ANY)
     fo, bo = pl.pallas_call(
         kernel,
         name="relay",
         out_shape=(jax.ShapeDtypeStruct(shape, BF), jax.ShapeDtypeStruct(shape, BF)),
-        in_specs=[vmem] * 4 + [anywhere] * 3 + [vmem] + [anywhere] * 3,
+        in_specs=[anywhere] * 11,
         out_specs=(anywhere, anywhere),
         scratch_shapes=[
             pltpu.VMEM((D, FE), BF),
@@ -619,11 +653,14 @@
             pltpu.VMEM((448, FE), BF),
             pltpu.VMEM((448, FE), F32),
             pltpu.VMEM((448, 448), BF),
-            pltpu.VMEM((128, 128), BF),
-            pltpu.VMEM((128, 128), BF),
             pltpu.VMEM((2, 8, 128, 256), BF),
             pltpu.VMEM((2, 2, 8, 128, 256), BF),
             pltpu.VMEM((8, 128), F32),
+            pltpu.VMEM((2, 128), jnp.int32),
+            pltpu.VMEM((2, 128), F32),
+            pltpu.VMEM((2, 128), jnp.int32),
+            pltpu.VMEM((2, 128), F32),
+            pltpu.VMEM((1, D), BF),
             dma((2,)),
             dma((2,)),
             dma((3, 2, 6)),
@@ -642,6 +679,7 @@
             dma((3,)),
             dma((3,)),
             dma((3, 2)),
+            dma((5,)),
         ],
         compiler_params=pltpu.CompilerParams(
             collective_id=0, has_side_effects=True, vmem_limit_bytes=64 * 1024 * 1024 - 65536

time: 187 us -> 185 us (0.989)
  no operation moved by 1% of the time
where the time goes in v4:
time: 185 us; the launch traced here: 183 us
  Pallas kernels  183 us (99%)
    pallas_call x1, Pallas kernels, local(): pl.pallas_call(kernel, name='relay', out_shape=(jax.ShapeDtypeStruct(shap...  180 us

profile of v4, /device:TPU:0, one launch (start us, length us, event | category | flops | bytes accessed | tf_op | source)
XLA Modules:
  0.0 183.5 jit_solution(9538397613075878093)
XLA Ops:
  0.6 180.4 %relay.1 = (bf16[8,16,3584]{2,1,0:T(8,128)(2,1)}, bf16[8,16,3584]{2,1,0:T(8,128)(2,1)}) custom-call(s32[2,128]{1,0:T(2,128)} %bitcast.28, f32[2,128]{1,0:T(2,128)} %bitcast.29, s32[2,128]{1,0:T(2,128)} %bitcast.30, f32[2,128]{1,0:T(2,128)} %bitcast.31, bf16[8,16,3584]{2,1,0:T(8,128)(2,1)} %bitcast.23, bf16[8,16,3584]{2,1,0:T(8,128)(2,1)} %bitcast.24, ...), custom_call_target="tpu_custom_call" | custom-call | flops 46000001024 | bytes 30000000 | tf_op jit(solution)/shard_map/relay/pallas_call | solution.py:633
  181.0 2.3 %results.1 = (bf16[8,16,3584]{2,1,0:T(8,128)(2,1)}, bf16[8,16,3584]{2,1,0:T(8,128)(2,1)}) custom-call(bf16[8,16,3584]{2,1,0:T(8,128)(2,1)} %get-tuple-element.6.fo, bf16[8,16,3584]{2,1,0:T(8,128)(2,1)} %get-tuple-element.7.bo), custom_call_target="tpu_custom_call" | custom-call | bytes 4000000 | tf_op jit(solution)/shard_map/results/pallas_call | solution.py:701

commit v5 on v4

--- a/solution.py
+++ b/solution.py
@@ -480,26 +480,38 @@
                 wait(B.at[h, 4 + other], s_c_r.at[n, h, 0])
                 wait(B.at[h, 4 + core], s_c_r.at[n, h, 1])
 
+    def pieces(ch):
+        return 2 if ch == len(CHUNKS) - 1 else 1
+
+    def piece(ch, part):
+        size = 8 // pieces(ch)
+        return (2 if part == 1 else len(CHUNKS) + ch), pl.ds(size * part, size)
+
     def relay_direct(ch):
         n, here, to, B = meta(1, ch)
         for h in (0, 1):
             wait(G.at[1, h, pl.ds(0, 7), :, :, here], s_r_r.at[n, h])
-        for d, base in ((2, 6), (1, 0), (3, 2)):
-            for h in (0, 1):
-                combine(1, ch, h, (d,))
-                for k in (0, 1):
-                    ss, rs = (s_t1_s.at[n, h], s_t1_r.at[n, h, 0]) if d == 2 else (s_t2_s.at[n, h], s_t2_r.at[n, h])
-                    send(S.at[to, h, 2 * at(h, d) + k, :, :, here], B.at[h, base + core, :, :, here], ss, rs, dev(h, d, k))
+        for part in range(pieces(ch)):
+            m, some = piece(ch, part)
+            for d, base in ((2, 6), (1, 0), (3, 2)):
+                for h in (0, 1):
+                    if part == 0:
+                        combine(1, ch, h, (d,))
+                    for k in (0, 1):
+                        ss, rs = (s_t1_s.at[m, h], s_t1_r.at[m, h, 0]) if d == 2 else (s_t2_s.at[m, h], s_t2_r.at[m, h])
+                        send(S.at[to, h, 2 * at(h, d) + k, some, :, here], B.at[h, base + core, some, :, here], ss, rs, dev(h, d, k))
         for h in (0, 1):
             own_start(1, ch, h, (0,))
 
-    def near_finish(b, ch, h):
-        n, here, to, B = meta(b, ch)
-        if b == 1 and ch in DIRECT:
-            wait(B.at[h, pl.ds(6, 2), :, :, here], s_t1_r.at[n, h, 0])
-        wait(B.at[h, pl.ds(0, 4), :, :, here], s_t2_r.at[n, h])
-        wait(B.at[h, 4 + other, :, :, here], s_c_r.at[n, h, 0])
-        wait(B.at[h, 4 + core, :, :, here], s_c_r.at[n, h, 1])
+    def near_finish(ch, h, part):
+        n, here, to, B = meta(1, ch)
+        m, some = piece(ch, part)
+        if ch in DIRECT:
+            wait(B.at[h, pl.ds(6, 2), some, :, here], s_t1_r.at[m, h, 0])
+        wait(B.at[h, pl.ds(0, 4), some, :, here], s_t2_r.at[m, h])
+        if part == 0:
+            wait(B.at[h, 4 + other, :, :, here], s_c_r.at[n, h, 0])
+            wait(B.at[h, 4 + core, :, :, here], s_c_r.at[n, h, 1])
 
     def arrived(b, h, q, k, here, direct=False):
         B = land(b)
@@ -536,19 +548,22 @@
     def forward_last(ch):
         c0, cw = CHUNKS[ch]
         n, here, to, B = meta(1, ch)
-        for h in (0, 1):
-            near_finish(1, ch, h)
-
-            def body(k, carry):
+        size = 8 // pieces(ch)
+        for part in range(pieces(ch)):
+            some = pl.ds(size * part, size)
+            for h in (0, 1):
+                near_finish(ch, h, part)
+
+                def body(k, carry):
+                    for q in (0, 1):
+                        spot = pl.ds(h * HALF + q * QUARTER + c0, cw)
+                        OWN[2, k, :, spot] = (OWN[2, k, :, spot].astype(F32) + arrived(1, h, q, k, here, ch in DIRECT)).astype(BF)
+                    return carry
+
+                lax.fori_loop(size * part, size * part + size, body, 0)
                 for q in (0, 1):
                     spot = pl.ds(h * HALF + q * QUARTER + c0, cw)
-                    OWN[2, k, :, spot] = (OWN[2, k, :, spot].astype(F32) + arrived(1, h, q, k, here, ch in DIRECT)).astype(BF)
-                return carry
-
-            lax.fori_loop(0, 8, body, 0)
-            for q in (0, 1):
-                spot = pl.ds(h * HALF + q * QUARTER + c0, cw)
-                send(OWN.at[2, :, :, spot], fo.at[:, :, spot], s_y_s.at[1 + ch], s_y_r.at[1 + ch], ahead)
+                    send(OWN.at[2, some, :, spot], fo.at[some, :, spot], s_y_s.at[1 + ch], s_y_r.at[1 + ch], ahead)
 
     def backward_last(k, carry):
         summed = jnp.concatenate([arrived(0, h, q, k, pl.ds(0, QUARTER)) for h in (0, 1) for q in (0, 1)], axis=1)
@@ -588,10 +603,18 @@
             n, here, to, B = meta(b, ch)
             for h in (0, 1):
                 wait(S.at[to, h, pl.ds(0, 7), pl.ds(0, 7), :, here], s_r_s.at[n, h])
-                wait(S.at[to, h, pl.ds(0, 2), :, :, here], s_t1_s.at[n, h])
-                wait(S.at[to, h, pl.ds(0, 5 if b == 1 else 1 + PARTS[0][1]), :, :, here], s_t2_s.at[n, h])
                 if b == 0:
+                    wait(S.at[to, h, pl.ds(0, 2)], s_t1_s.at[n, h])
+                    wait(S.at[to, h, pl.ds(0, 1 + PARTS[0][1])], s_t2_s.at[n, h])
                     wait(S.at[to, h, pl.ds(0, PARTS[1][1])], s_t2_s.at[1, h])
+                elif pieces(ch) == 1:
+                    wait(S.at[to, h, pl.ds(0, 2), :, :, here], s_t1_s.at[n, h])
+                    wait(S.at[to, h, pl.ds(0, 5), :, :, here], s_t2_s.at[n, h])
+                else:
+                    wait(S.at[to, h, pl.ds(0, 1), :, :, here], s_t1_s.at[n, h])
+                    wait(S.at[to, h, pl.ds(0, 3), :, :, here], s_t2_s.at[n, h])
+                    wait(S.at[to, h, pl.ds(0, 1), :, :, here], s_t1_s.at[2, h])
+                    wait(S.at[to, h, pl.ds(0, 2), :, :, here], s_t2_s.at[2, h])
     wait(bo, s_y_s.at[0])
     wait(bo, s_y_r.at[0])
     for ch, (c0, cw) in enumerate(CHUNKS):

time: 185 us -> 184 us (level)
  no operation moved by 1% of the time
where the time goes in v5:
time: 184 us; the launch traced here: 183 us
  Pallas kernels  182 us (99%)
    pallas_call x1, Pallas kernels, local(): pl.pallas_call(kernel, name='relay', out_shape=(jax.ShapeDtypeStruct(shap...  180 us

profile of v5, /device:TPU:0, one launch (start us, length us, event | category | flops | bytes accessed | tf_op | source)
XLA Modules:
  0.0 182.9 jit_solution(16650135416503265419)
XLA Ops:
  0.6 179.8 %relay.1 = (bf16[8,16,3584]{2,1,0:T(8,128)(2,1)}, bf16[8,16,3584]{2,1,0:T(8,128)(2,1)}) custom-call(s32[2,128]{1,0:T(2,128)} %bitcast.28, f32[2,128]{1,0:T(2,128)} %bitcast.29, s32[2,128]{1,0:T(2,128)} %bitcast.30, f32[2,128]{1,0:T(2,128)} %bitcast.31, bf16[8,16,3584]{2,1,0:T(8,128)(2,1)} %bitcast.23, bf16[8,16,3584]{2,1,0:T(8,128)(2,1)} %bitcast.24, ...), custom_call_target="tpu_custom_call" | custom-call | flops 46000001024 | bytes 30000000 | tf_op jit(solution)/shard_map/relay/pallas_call | solution.py:656
  180.4 2.3 %results.1 = (bf16[8,16,3584]{2,1,0:T(8,128)(2,1)}, bf16[8,16,3584]{2,1,0:T(8,128)(2,1)}) custom-call(bf16[8,16,3584]{2,1,0:T(8,128)(2,1)} %get-tuple-element.6.fo, bf16[8,16,3584]{2,1,0:T(8,128)(2,1)} %get-tuple-element.7.bo), custom_call_target="tpu_custom_call" | custom-call | bytes 4000000 | tf_op jit(solution)/shard_map/results/pallas_call | solution.py:724
